TPU v7x, 512 devices: a whole 4x8x8 slice. The times are simulated.
512 devices in a mesh: space: 128 (over z, y, core), pair: 4 (over x).
Axes of the slice: x: 4, y: 8, z: 8, core: 2. Of those that a mesh axis runs over, the one named last changes fastest.
Arguments:
- positions: float32 [3, 262144], P(None, 'space'), may hold values from -1 to 1296, as said below
- polarizability: float32 [262144], P('space'), may hold values from 0.4 to 1.6
- charges: float32 [262144], P('space'), may hold values from -4 to 4
- groups: int32 [262144], P('space'), may hold values from 0 to 87380, never falling along the last dimension, each value on 1 to 6 neighbouring positions
- pair_list: int32 [128, 64, 2], P('space'), may hold values from 0 to 1023, as said below
- tile_count: int32 [128], P('space'), may hold values from 8 to 64, as said below
Outputs:
- dipoles: float32 [3, 262144], P(None, ('space', 'pair'))
- residual: float32 [3, 262144], P(None, ('space', 'pair'))
Inputs may be any that keep to these rules, and one draw needn't show every extreme that they name: `positions`: Positions: block c sits on a lattice of spacing 2.15 in the cell of its row and column, with small displacements of each atom; no two atoms are closer than 1.2. `pair_list`: for entries t < tile_count[o]: column 0 is a slot 0 to 7 of row o; the partner's row is o, o + 1 or o + 2, and its column differs from the slot by at most one, counted around 8; with partner row o it is the slot itself or the next column. Each slot lists itself, and no pair twice. Entries at and after the count are padding. `tile_count`: number of listed entries of each row; some row lists all 64 candidate tiles.
All inputs are finite; a program needn't handle non-finite values.
Results may differ from a plain program's by a relative error of at most 0.00055.
Values sent between devices are 32-bit elements; how exact they have to be, the bound alone decides.
A program may use at most 64 MiB of HBM per device.

v0:
```python
import jax
import jax.numpy as jnp
from jax import lax
from jax.sharding import PartitionSpec as P

BLK = 256
BPD = 8
ITERS = 3


spacing = 2.15
thole_a = 0.39


def shifted(value, axis, steps):
    count = lax.axis_size(axis)
    first, last = (max(0, -steps), min(count, count - steps))
    return lax.ppermute(value, axis, [(source, source + steps) for source in range(first, last)])


def column_wrap(own_column, far_column):
    column_diff = far_column - own_column
    return (column_diff < -1).astype(jnp.int32) - (column_diff > 1).astype(jnp.int32)


def tile_terms(pos_i, pos_j, alpha_i, alpha_j, image_shift, self_tile):
    period = BPD * 8 * spacing
    offset = jnp.array([1.0, 0.0, 0.0], jnp.float32)[:, None] * (
        image_shift.astype(jnp.float32) * period
    )
    displacement = pos_i[:, :, None] - (pos_j + offset)[:, None, :]
    squared = jnp.sum(displacement * displacement, 0)
    excluded = jnp.eye(pos_i.shape[1], dtype=jnp.float32) * self_tile
    padded_sq = squared + excluded
    inverse = lax.rsqrt(padded_sq)
    distance = padded_sq * inverse
    damp_radius = (alpha_i[:, None] * alpha_j[None, :]) ** (1.0 / 6.0)
    scaled = distance / damp_radius
    damping = thole_a * scaled * scaled * scaled
    decayed = jnp.exp(-damping)
    third_order = -jnp.expm1(-damping)
    fifth_order = third_order - damping * decayed
    retained = 1.0 - excluded
    inverse_cube = inverse * inverse * inverse
    coef_three = retained * third_order * inverse_cube
    coef_five = retained * 3.0 * fifth_order * inverse_cube * inverse * inverse
    return (displacement, coef_three, coef_five)


def charge_pair(displacement, coef_three, charge_i, charge_j, group_mask):
    weighted = coef_three * group_mask
    near_field = jnp.sum(displacement * (weighted * charge_j[None, :])[None], 2)
    far_field = -jnp.sum(displacement * (weighted * charge_i[:, None])[None], 1)
    return (near_field, far_field)


def dipole_pair(displacement, coef_three, coef_five, dipole_i, dipole_j):
    along_j = jnp.sum(displacement * dipole_j[:, None, :], 0)
    near_field = jnp.sum((coef_five * along_j)[None] * displacement, 2) - jnp.sum(
        coef_three[None] * dipole_j[:, None, :], 2
    )
    along_i = jnp.sum(displacement * dipole_i[:, :, None], 0)
    far_field = jnp.sum((coef_five * along_i)[None] * displacement, 1) - jnp.sum(
        coef_three[None] * dipole_i[:, :, None], 1
    )
    return (near_field, far_field)


def add_block(window_field, update, start):
    current = lax.dynamic_slice_in_dim(window_field, start, update.shape[1], 1)
    return lax.dynamic_update_slice_in_dim(window_field, current + update, start, 1)


def precond_sum(first_vec, second_vec):
    return lax.psum(jnp.sum(first_vec * second_vec), ("space", "pair"))


def on_device(positions, polarizability, charges, groups, pair_list, tile_count):
    owner_index = lax.axis_index("space")
    pair_index = lax.axis_index("pair")
    pair_count = lax.axis_size("pair")
    owned_atoms = positions.shape[1]
    blocks = owned_atoms // BLK
    share_size = owned_atoms // pair_count
    local_attrs = jnp.concatenate(
        [positions, polarizability[None], charges[None], groups.astype(jnp.float32)[None]], 0
    )
    ahead_attrs = [shifted(local_attrs, "space", -offset) for offset in (1, 2)]
    window_attrs = jnp.concatenate([local_attrs] + ahead_attrs, 1)
    alpha_share = lax.dynamic_slice_in_dim(polarizability, pair_index * share_size, share_size)[
        None, :
    ]
    span_size = pair_list.shape[1] // pair_count
    listed = tile_count[0]
    first_tile = pair_index * span_size
    stride = 1
    visits = jnp.clip(listed - first_tile, 0, span_size)

    def sweep(window_vals, charged):

        def visit(sweep_step, window_field):
            tile_row = first_tile + sweep_step * stride
            own_slot = pair_list[0, tile_row, 0]
            partner = pair_list[0, tile_row, 1]
            far_slot = partner - owner_index * blocks
            own_attrs = lax.dynamic_slice_in_dim(window_attrs, own_slot * BLK, BLK, 1)
            far_attrs = lax.dynamic_slice_in_dim(window_attrs, far_slot * BLK, BLK, 1)
            self_tile = (far_slot == own_slot).astype(jnp.float32)
            image_shift = column_wrap(own_slot, partner % blocks)
            displacement, coef_three, coef_five = tile_terms(
                own_attrs[:3], far_attrs[:3], own_attrs[3], far_attrs[3], image_shift, self_tile
            )
            if charged:
                group_mask = (own_attrs[5][:, None] != far_attrs[5][None, :]).astype(jnp.float32)
                near_field, far_field = charge_pair(
                    displacement, coef_three, own_attrs[4], far_attrs[4], group_mask
                )
            else:
                own_dipoles = lax.dynamic_slice_in_dim(window_vals, own_slot * BLK, BLK, 1)
                far_dipoles = lax.dynamic_slice_in_dim(window_vals, far_slot * BLK, BLK, 1)
                near_field, far_field = dipole_pair(
                    displacement, coef_three, coef_five, own_dipoles, far_dipoles
                )
            window_field = add_block(window_field, near_field, own_slot * BLK)
            return add_block(window_field, far_field * (1.0 - self_tile), far_slot * BLK)

        zeroed = jnp.zeros((3, window_attrs.shape[1]), jnp.float32)
        return lax.fori_loop(0, visits, visit, zeroed)

    def spread(share_vals):
        whole_block = lax.all_gather(share_vals, "pair", axis=1, tiled=True)
        ahead_blocks = [shifted(whole_block, "space", -offset) for offset in (1, 2)]
        return jnp.concatenate([whole_block] + ahead_blocks, 1)

    def collect(window_field):
        own_field = window_field[:, :owned_atoms]
        for offset in (1, 2):
            own_field = own_field + shifted(
                window_field[:, offset * owned_atoms : (offset + 1) * owned_atoms], "space", offset
            )
        return lax.psum_scatter(own_field, "pair", scatter_dimension=1, tiled=True)

    def field_of(share_vals):
        return collect(sweep(spread(share_vals), False))

    direct_field = collect(sweep(None, True))
    dipoles = alpha_share * direct_field
    residual = field_of(dipoles)
    precond = alpha_share * residual
    direction = precond
    rz_value = precond_sum(residual, precond)
    for iteration in range(ITERS):
        image_vec = direction / alpha_share - field_of(direction)
        curvature_sum = lax.psum(jnp.sum(direction * image_vec), ("space", "pair"))
        length = rz_value / curvature_sum
        dipoles = dipoles + length * direction
        residual = residual - length * image_vec
        if iteration + 1 < ITERS:
            precond = alpha_share * residual
            rz_next = precond_sum(residual, precond)
            direction = precond + rz_next / rz_value * direction
            rz_value = rz_next
    return (dipoles, residual)


def solution(mesh):
    return jax.shard_map(
        on_device,
        mesh=mesh,
        in_specs=(
            P(None, "space"),
            P("space"),
            P("space"),
            P("space"),
            P("space", None, None),
            P("space"),
        ),
        out_specs=(P(None, ("space", "pair")), P(None, ("space", "pair"))),
        check_vma=False,
    )
```

profile of v0, /device:TPU:1, one launch (start us, length us, event | category | flops | bytes accessed | tf_op | source)
XLA Modules:
  0.0 1353.6 jit_solution(4045247360240852999)
XLA Ops:
  7.9 0.9 pad_maximum_fusion.5
  8.8 8.8 collective-permute-start
  17.6 1.3 collective-permute-start.1
  19.6 3.7 collective-permute-done.1
  24.0 97.6 %while.70 = (s32[]{:T(128)}, f32[3,6144]{1,0:T(4,128)S(1)}, s32[]{:T(128)}, s32[]{:T(128)}, s32[1,64,2]{1,2,0:T(2,128)S(1)}, /*index=5*/f32[6,6144]{1,0:T(8,128)...) while((s32[]{:T(128)}, f32[3,6144]{1,0:T(4,128)S(1)}, ...), condition=%wide.region_4.5_spmd.clone, body=%wide.region_0.4_spmd.sunk.clone.sunk | while | flops 2820395 | bytes 1647278 | solution.py:128
  121.7 1.9 collective-permute-start.2
  123.6 1.4 collective-permute-start.3
  125.0 1.0 collective-permute-done.3
  126.0 1.4 copy.13
  127.5 30.7 %reduce-scatter.16.cloned.1.call-done = f32[512,3]{1,0:T(8,128)} async-done(((f32[2048,3]{1,0:T(8,128)}), f32[512,3]{1,0:T(8,128)}) %reduce-scatter.16.cloned.1.call-update) | async-done | bytes 6160
  158.2 1.1 copy.14
  159.3 9.3 all_gather.12
  168.6 7.2 collective-permute-start.4
  175.8 1.3 collective-permute-start.5
  177.1 1.4 collective-permute-done.4
  178.5 2.5 collective-permute-done.5
  181.1 114.7 %while.71 = (s32[]{:T(128)}, f32[3,6144]{1,0:T(4,128)S(1)}, s32[]{:T(128)}, s32[]{:T(128)}, s32[1,64,2]{1,2,0:T(2,128)S(1)}, /*index=5*/s32[]{:T(128)}, f32[6,61...) while((s32[]{:T(128)}, f32[3,6144]{1,0:T(4,128)S(1)}, ...), condition=%wide.region_14.15_spmd.clone, body=%wide.region_6.14_spmd.sunk.clone.sunk | while | flops 5703209 | bytes 3510922 | solution.py:128
  295.8 3.6 collective-permute-start.6
  299.4 3.1 collective-permute-start.7
  302.6 1.0 collective-permute-done.7
  303.6 1.4 copy.15
  305.0 28.5 %reduce-scatter.18.cloned.1.call-done = f32[512,3]{1,0:T(8,128)} async-done(((f32[2048,3]{1,0:T(8,128)}), f32[512,3]{1,0:T(8,128)}) %reduce-scatter.18.cloned.1.call-update) | async-done | bytes 6160
  333.5 1.1 copy.16
  334.6 9.0 all_gather.13
  343.6 6.8 collective-permute-start.8
  350.4 1.3 collective-permute-start.9
  351.7 1.4 collective-permute-done.8
  353.1 2.6 collective-permute-done.9
  355.7 114.7 %while.72 = (s32[]{:T(128)}, f32[3,6144]{1,0:T(4,128)S(1)}, s32[]{:T(128)}, s32[]{:T(128)}, s32[1,64,2]{1,2,0:T(2,128)S(1)}, /*index=5*/s32[]{:T(128)}, f32[6,61...) while((s32[]{:T(128)}, f32[3,6144]{1,0:T(4,128)S(1)}, ...), condition=%wide.region_26.27_spmd.clone, body=%wide.region_18.26_spmd.sunk.clone.sunk | while | flops 5703209 | bytes 3510922 | solution.py:128
  470.4 3.6 collective-permute-start.10
  474.0 3.1 collective-permute-start.11
  477.2 1.0 collective-permute-done.11
  478.2 1.4 copy.17
  479.6 28.5 %reduce-scatter.20.cloned.1.call-done = f32[512,3]{1,0:T(8,128)} async-done(((f32[2048,3]{1,0:T(8,128)}), f32[512,3]{1,0:T(8,128)}) %reduce-scatter.20.cloned.1.call-update) | async-done | bytes 6160
  508.1 1.1 copy.18
  509.8 98.7 %all-reduce = (f32[]{:T(128)}, f32[]{:T(128)}) all-reduce(f32[]{:T(128)} %get-tuple-element.924, f32[]{:T(128)} %get-tuple-element.923), channel_id=1, replica_groups=mesh['space'=128,'pair'=4] {'space','pair'}, use_global_device_ids=true, to_apply=%region_17.18 | all-reduce | flops 2 | bytes 16 | tf_op jit(solution)/shard_map/psum | solution.py:75
  610.5 95.7 %psum.44 = f32[]{:T(128)} all-reduce(f32[]{:T(128)} %get-tuple-element.1007), channel_id=1, replica_groups=mesh['space'=128,'pair'=4] {'space','pair'}, use_global_device_ids=true, to_apply=%region_31.32 | all-reduce | flops 1 | bytes 8 | tf_op jit(solution)/shard_map/psum | solution.py:75
  707.7 9.0 all_gather.14
  716.7 5.4 collective-permute-start.12
  722.1 1.3 collective-permute-start.13
  723.4 1.2 collective-permute-done.12
  724.6 2.5 collective-permute-done.13
  727.2 114.6 %while.73 = (s32[]{:T(128)}, f32[3,6144]{1,0:T(4,128)S(1)}, s32[]{:T(128)}, s32[]{:T(128)}, s32[1,64,2]{1,2,0:T(2,128)S(1)}, /*index=5*/s32[]{:T(128)}, f32[6,61...) while((s32[]{:T(128)}, f32[3,6144]{1,0:T(4,128)S(1)}, ...), condition=%wide.region_40.41_spmd.clone, body=%wide.region_32.40_spmd.sunk.clone.sunk | while | flops 5703209 | bytes 3510922 | solution.py:128
  841.8 3.6 collective-permute-start.14
  845.4 3.1 collective-permute-start.15
  848.5 1.0 collective-permute-done.15
  849.5 1.4 copy.19
  851.0 25.4 %reduce-scatter.22.cloned.1.call-done = f32[512,3]{1,0:T(8,128)} async-done(((f32[2048,3]{1,0:T(8,128)}), f32[512,3]{1,0:T(8,128)}) %reduce-scatter.22.cloned.1.call-update) | async-done | bytes 6160
  876.4 1.1 copy.20
  878.1 98.8 %psum.45 = f32[]{:T(128)} all-reduce(f32[]{:T(128)} %multiply_reduce_fusion.9), channel_id=1, replica_groups=mesh['space'=128,'pair'=4] {'space','pair'}, use_global_device_ids=true, to_apply=%region_43.44 | all-reduce | flops 1 | bytes 8 | tf_op jit(solution)/shard_map/psum | solution.py:154
  978.9 95.7 %psum.46 = f32[]{:T(128)} all-reduce(f32[]{:T(128)} %get-tuple-element.1005), channel_id=1, replica_groups=mesh['space'=128,'pair'=4] {'space','pair'}, use_global_device_ids=true, to_apply=%region_45.46 | all-reduce | flops 1 | bytes 8 | tf_op jit(solution)/shard_map/psum | solution.py:75
  1076.0 9.0 all_gather.15
  1085.0 5.4 collective-permute-start.16
  1090.4 1.3 collective-permute-start.17
  1091.7 1.3 collective-permute-done.16
  1093.0 2.4 collective-permute-done.17
  1095.5 114.6 %while.74 = (s32[]{:T(128)}, f32[3,6144]{1,0:T(4,128)S(1)}, s32[]{:T(128)}, s32[]{:T(128)}, s32[1,64,2]{1,2,0:T(2,128)S(1)}, /*index=5*/s32[]{:T(128)}, f32[6,61...) while((s32[]{:T(128)}, f32[3,6144]{1,0:T(4,128)S(1)}, ...), condition=%wide.region_54.55_spmd.clone, body=%wide.region_46.54_spmd.sunk.clone.sunk | while | flops 5703209 | bytes 3510922 | solution.py:128
  1210.1 3.7 collective-permute-start.18
  1213.9 3.1 collective-permute-start.19
  1216.9 1.0 collective-permute-done.19
  1217.9 1.4 copy.21
  1219.3 24.8 %reduce-scatter.24.cloned.1.call-done = f32[512,3]{1,0:T(8,128)} async-done(((f32[2048,3]{1,0:T(8,128)}), f32[512,3]{1,0:T(8,128)}) %reduce-scatter.24.cloned.1.call-update) | async-done | bytes 6160
  1244.1 1.1 copy.22
  1245.8 99.3 %psum.47 = f32[]{:T(128)} all-reduce(f32[]{:T(128)} %multiply_reduce_fusion.8), channel_id=1, replica_groups=mesh['space'=128,'pair'=4] {'space','pair'}, use_global_device_ids=true, to_apply=%region_57.58 | all-reduce | flops 1 | bytes 8 | tf_op jit(solution)/shard_map/psum | solution.py:154
  (906 shorter events, 201.6 us)
Async XLA Ops:
  7.2 0.8 copy-start.2
  7.2 0.8 copy-start.3
  7.2 151.1 %reduce-scatter.16.cloned.1.call-start = ((), (), s32[]{:S(2)}) async-start(), calls=%async_computation.5 | async-start | bytes 1310720
  7.9 15.4 %copy-start.1 = (f32[3,2048]{1,0:T(4,128)S(1)}, f32[3,2048]{1,0:T(4,128)}, u32[]{:S(2)}) copy-start(f32[3,2048]{1,0:T(4,128)} %param.21) | copy-start | bytes 73732
  8.8 10.8 collective-permute-start
  17.6 5.7 collective-permute-start.1
  23.3 0.7 copy-start
  23.4 0.7 copy-start.4
  121.7 3.3 collective-permute-start.2
  123.6 2.4 collective-permute-start.3
  127.4 206.1 %reduce-scatter.18.cloned.1.call-start = ((), (), s32[]{:S(2)}) async-start(), calls=%async_computation.6 | async-start | bytes 1310720
  168.6 9.9 collective-permute-start.4
  175.8 5.3 collective-permute-start.5
  295.8 6.8 collective-permute-start.6
  299.4 4.1 collective-permute-start.7
  305.0 203.1 %reduce-scatter.20.cloned.1.call-start = ((), (), s32[]{:S(2)}) async-start(), calls=%async_computation.7 | async-start | bytes 1310720
  343.6 9.5 collective-permute-start.8
  350.4 5.3 collective-permute-start.9
  470.4 6.7 collective-permute-start.10
  474.0 4.2 collective-permute-start.11
  479.6 396.8 %reduce-scatter.22.cloned.1.call-start = ((), (), s32[]{:S(2)}) async-start(), calls=%async_computation.8 | async-start | bytes 1310720
  716.7 7.9 collective-permute-start.12
  722.1 5.0 collective-permute-start.13
  841.8 6.7 collective-permute-start.14
  845.4 4.1 collective-permute-start.15
  850.9 393.2 %reduce-scatter.24.cloned.1.call-start = ((), (), s32[]{:S(2)}) async-start(), calls=%async_computation.9 | async-start | bytes 1310720
  1085.0 8.0 collective-permute-start.16
  1090.4 5.0 collective-permute-start.17
  1210.1 6.8 collective-permute-start.18
  1213.9 4.1 collective-permute-start.19
Sparse Core Ops, SparseCore 0:
  127.5 30.6 reduce-scatter.15
  305.1 28.3 reduce-scatter.17
  479.7 28.3 reduce-scatter.19
  851.0 25.3 reduce-scatter.21
  1219.4 24.5 reduce-scatter.23
where the time goes:
time: 1360 us; the launch traced here: 1350 us
  blocking collectives  525 us (39%)
  loops' own time  360 us (26%)
  waiting for transfers between devices  162 us (12%)
  other arithmetic  142 us (10%)
  local copies, waits for them, and re-layouts  71.8 us (5%)
  starting transfers between devices  70.5 us (5%)
  between operations  21.7 us (2%)
    another operation x5, loops' own time, sweep(): return lax.fori_loop(0, visits, visit, zeroed)  360 us
    psum x3, blocking collectives, precond_sum(): return lax.psum(jnp.sum(first_vec * second_vec), ('space', 'pair'))  290 us
    psum x2, blocking collectives, on_device(): curvature_sum = lax.psum(jnp.sum(direction * image_vec), ('space', 'pair'))  198 us
    unnamed x10, waiting for transfers between devices  138 us
    ppermute x20, starting transfers between devices, shifted(): lax.ppermute(value, axis, [(source, source + steps) for source in range(f...  70.3 us
    dynamic_slice x80, local copies, waits for them, and re-layouts, visit(): partner = pair_list[0, tile_row, 1]  52.1 us
    all_gather x4, blocking collectives, spread(): whole_block = lax.all_gather(share_vals, 'pair', axis=1, tiled=True)  36.4 us
    mul x64, other arithmetic, dipole_pair(): coef_five * along_j  28.8 us
  transfers between devices with their start and end apart: 25, of which 19 were waited for; matrix products, arithmetic and copies ran while one was open for 0% of the time, Pallas kernels for 0%

commit v1 on v0

v1 whole, which is shorter than its diff:
```python
import functools

import jax
import jax.numpy as jnp
from jax import lax
from jax.experimental import pallas as pl
from jax.experimental.pallas import tpu as pltpu
from jax.sharding import PartitionSpec as P

BLK = 256
BPD = 8
ITERS = 3
LANES = 128
ROWS = 32
GROUPS = BLK // ROWS
PERIOD = BPD * 8 * 2.15
THOLE = 0.39
SWEEPS = ITERS + 1
MESH = pl.DeviceIdType.MESH

HALO = [(d, e) for d in (-2, -1, 0, 1, 2) for e in (-1, 0, 1) if (d, e) != (0, 0)]
AHEAD = [-2, -1, 1, 2]
GRAM = [(i, j) for i in range(ITERS) for j in range(i, ITERS + 1)]


def kernel(
    spaces,
    pairs,
    span_y,
    attr_ref,
    dip_ref,
    res_ref,
    window,
    column,
    weight,
    coef,
    acc,
    alpha,
    direct,
    vec,
    field,
    gram,
    send_sem,
    recv_sem,
):
    sp = lax.axis_index("space")
    pr = lax.axis_index("pair")
    core = lax.rem(sp, 2)
    y = lax.rem(sp // 2, span_y)
    z = sp // (2 * span_y)
    span_z = spaces // (2 * span_y)

    def at_space(d):
        return lax.rem(sp + (d + spaces), spaces)

    def at_pair(e):
        return lax.rem(pr + (e + pairs), pairs)

    def at_core(c):
        return sp - core + lax.rem(core + c, 2)

    stages = [
        (
            [(at_core(c), at_pair(k)) for k in range(pairs) for c in range(2) if (k, c) != (0, 0)],
            pr * 2 + core,
        ),
        (
            [(sp + (lax.rem(y + k, span_y) - y) * 2, pr) for k in range(1, span_y)],
            y,
        ),
        (
            [(sp + (lax.rem(z + k, span_z) - z) * 2 * span_y, pr) for k in range(1, span_z)],
            z,
        ),
    ]

    barrier = pltpu.get_barrier_semaphore()
    partners = [(at_space(d), at_pair(e)) for d, e in HALO]
    for members, _ in stages:
        partners = partners + members
    for partner in partners:
        pl.semaphore_signal(barrier, inc=1, device_id=partner, device_id_type=MESH)

    for k in range(4):
        block = lax.rem(2 * pr + (k - 1 + BPD), BPD)
        window[2, :, k * BLK : (k + 1) * BLK] = attr_ref[
            :, pl.ds(pl.multiple_of(block * BLK, BLK), BLK)
        ]
    low = jnp.where(pr == 0, -PERIOD, 0.0).astype(jnp.float32)
    high = jnp.where(pr == pairs - 1, PERIOD, 0.0).astype(jnp.float32)
    window[2, 0:1, 0:BLK] = window[2, 0:1, 0:BLK] + low
    window[2, 0:1, 3 * BLK :] = window[2, 0:1, 3 * BLK :] + high

    for a in range(2):
        for c in range(2):
            lanes = pl.ds((a + 1) * BLK + c * LANES, LANES)
            turned = window[2, 0:8, lanes].T
            for k, row in enumerate((0, 1, 2, 5, 6)):
                values = jnp.broadcast_to(turned[:, row : row + 1], (LANES, LANES))
                if row == 6:
                    values = values * THOLE
                column[a, k, c * LANES : (c + 1) * LANES, :] = values
            share = window[2, 3:4, lanes]
            for k in range(3):
                alpha[a, 2 * k + c : 2 * k + c + 1, :] = share
        alpha[a, 6:8, :] = jnp.zeros((2, LANES), jnp.float32)

    pl.semaphore_wait(barrier, len(partners))

    def attr_copy(index, d):
        return pltpu.make_async_remote_copy(
            src_ref=window.at[2],
            dst_ref=window.at[2 - d],
            send_sem=send_sem.at[index],
            recv_sem=recv_sem.at[index],
            device_id=(at_space(d), pr),
            device_id_type=MESH,
        )

    for index, d in enumerate(AHEAD):
        attr_copy(index, d).start()

    def weigh(a, row, step):
        slot = a * 15 + row * 3 + step
        dx = step - 1
        own, far = (a + 1) * BLK, (a + step) * BLK
        if row == 2:
            entry, lane = (8 + abs(dx), far if dx < 0 else own)
        elif row > 2:
            entry, lane = (8 + (2, 5)[row - 3] + dx + 1, own)
        else:
            entry, lane = (8 + (5, 2)[row] - dx + 1, far)
        source = 2 if row >= 2 else row
        weight[slot : slot + 1, :] = window[source, entry : entry + 1, lane : lane + LANES]

    def build(a, rows, row, step, c, totals, itself):
        lanes = pl.ds(pl.multiple_of((a + step) * BLK + c * LANES, LANES), LANES)

        def far(entry):
            return window[row, entry : entry + 1, lanes]

        rx = column[a, 0, rows, :] - far(0)
        ry = column[a, 1, rows, :] - far(1)
        rz = column[a, 2, rows, :] - far(2)
        squared = jnp.maximum(rx * rx + ry * ry + rz * rz, 1.0)
        inverse = lax.rsqrt(squared)
        inverse_sq = inverse * inverse
        damping = (squared * (squared * inverse)) * (column[a, 4, rows, :] * far(6))
        decayed = jnp.exp(-damping)
        third = 1.0 - decayed
        fifth = third - damping * decayed
        tile = a * 15 + row * 3 + step
        weighted = (inverse_sq * inverse) * weight[pl.ds(tile, 1), :]
        three = third * weighted
        five = (fifth * inverse_sq) * (weighted * 3.0)
        root = five * lax.rsqrt(jnp.maximum(five, 1e-30))
        index = tile * 2 + c
        coef[index, 0, rows, :] = rx * root
        coef[index, 1, rows, :] = ry * root
        coef[index, 2, rows, :] = rz * root
        if itself:
            shape = (ROWS, LANES)
            own = lax.broadcasted_iota(jnp.int32, shape, 0) + rows.start
            other = lax.broadcasted_iota(jnp.int32, shape, 1) + c * LANES
            coef[index, 3, rows, :] = jnp.where(own == other, 0.0, three)
        else:
            coef[index, 3, rows, :] = three
        charged = jnp.where(column[a, 3, rows, :] != far(5), three * far(4), 0.0)
        ex, ey, ez = totals
        return (ex + charged * rx, ey + charged * ry, ez + charged * rz)

    def apply(n, a, rows, row, step, c, totals):
        index = (a * 15 + row * 3 + step) * 2 + c
        sx, sy, sz, three = (coef[index, k, rows, :] for k in range(4))
        vx, vy, vz = (vec[n, row, a + step, 2 * k + c : 2 * k + c + 1, :] for k in range(3))
        along = sx * vx + sy * vy + sz * vz
        ex, ey, ez = totals
        return (
            ex + (along * sx - three * vx),
            ey + (along * sy - three * vy),
            ez + (along * sz - three * vz),
        )

    def zeros():
        return tuple(jnp.zeros((ROWS, LANES), jnp.float32) for _ in range(3))

    def place(group):
        a = group // GROUPS
        return a, pl.ds(pl.multiple_of((group - a * GROUPS) * ROWS, ROWS), ROWS)

    def load_acc(a, rows):
        return tuple(acc[a, k, rows, :] for k in range(3))

    def store_acc(a, rows, totals):
        for k in range(3):
            acc[a, k, rows, :] = totals[k]

    def summed(a):
        parts = []
        for k in range(3):
            for c in range(2):
                turned = acc[a, k, c * LANES : (c + 1) * LANES, :].T
                parts.append(jnp.sum(turned, axis=0, keepdims=True))
        parts.append(jnp.zeros((2, LANES), jnp.float32))
        return jnp.concatenate(parts, axis=0)

    for a in range(2):
        for step in range(3):
            for row in (2, 3, 4):
                weigh(a, row, step)

    def build_own(group, carry):
        a, rows = place(group)
        totals = zeros()
        for step in range(3):
            for c in range(2):
                totals = build(a, rows, 2, step, c, totals, step == 1)
        store_acc(a, rows, totals)
        return carry

    lax.fori_loop(0, 2 * GROUPS, build_own, 0)
    for index, d in enumerate(AHEAD):
        attr_copy(index, d).wait()
    for a in range(2):
        for step in range(3):
            for row in (0, 1):
                weigh(a, row, step)

    def build_rest(group, carry):
        a, rows = place(group)

        def one_row(index, totals):
            row = index + index // 2
            for step in range(3):
                for c in range(2):
                    totals = build(a, rows, row, step, c, totals, False)
            return totals

        store_acc(a, rows, lax.fori_loop(0, 4, one_row, load_acc(a, rows)))
        return carry

    lax.fori_loop(0, 2 * GROUPS, build_rest, 0)
    for a in range(2):
        value = summed(a)
        direct[a] = value
        vec[0, 2, a + 1] = value * alpha[a]

    base = len(AHEAD)

    def halo_copy(n, index):
        d, e = HALO[index]
        if e == 0:
            source = vec.at[n, 2, pl.ds(1, 2)]
            target = vec.at[n, 2 - d, pl.ds(1, 2)]
        elif e == 1:
            source = vec.at[n, 2, pl.ds(2, 1)]
            target = vec.at[n, 2 - d, pl.ds(0, 1)]
        else:
            source = vec.at[n, 2, pl.ds(1, 1)]
            target = vec.at[n, 2 - d, pl.ds(3, 1)]
        place_of = base + n * len(HALO) + index
        return pltpu.make_async_remote_copy(
            src_ref=source,
            dst_ref=target,
            send_sem=send_sem.at[place_of],
            recv_sem=recv_sem.at[place_of],
            device_id=(at_space(d), at_pair(e)),
            device_id_type=MESH,
        )

    def sweep(n, carry):
        for index in range(len(HALO)):
            halo_copy(n, index).start()

        def near(group, inner):
            a, rows = place(group)
            totals = zeros()
            for far in range(2):
                for c in range(2):
                    totals = apply(n, a, rows, 2, far + 1 - a, c, totals)
            store_acc(a, rows, totals)
            return inner

        lax.fori_loop(0, 2 * GROUPS, near, 0)
        for index in range(len(HALO)):
            halo_copy(n, index).wait()

        def rest(group, inner):
            a, rows = place(group)
            totals = load_acc(a, rows)
            for c in range(2):
                totals = apply(n, a, rows, 2, 2 * a, c, totals)

            def one_row(index, totals):
                row = index + index // 2
                for step in range(3):
                    for c in range(2):
                        totals = apply(n, a, rows, row, step, c, totals)
                return totals

            store_acc(a, rows, lax.fori_loop(0, 4, one_row, totals))
            return inner

        lax.fori_loop(0, 2 * GROUPS, rest, 0)
        for a in range(2):
            value = summed(a)
            field[n, a] = value
            vec[n + 1, 2, a + 1] = value * alpha[a]
        return carry

    lax.fori_loop(0, SWEEPS, sweep, 0)

    lines = []
    for i, j in GRAM:
        product = field[i, 0] * (alpha[0] * field[j, 0]) + field[i, 1] * (alpha[1] * field[j, 1])
        lines.append(jnp.sum(product, axis=0, keepdims=True))
    lines.append(jnp.zeros((16 - len(GRAM), LANES), jnp.float32))
    total = jnp.concatenate(lines, axis=0)
    first = base + SWEEPS * len(HALO)
    for stage, (members, mine) in enumerate(stages):
        gram[stage, mine] = total
        copies = []
        for index, member in enumerate(members):
            copies.append(
                pltpu.make_async_remote_copy(
                    src_ref=gram.at[stage, mine],
                    dst_ref=gram.at[stage, mine],
                    send_sem=send_sem.at[first + index],
                    recv_sem=recv_sem.at[first + index],
                    device_id=member,
                    device_id_type=MESH,
                )
            )
            copies[-1].start()
        for copy in copies:
            copy.wait()
        first += len(members)
        total = gram[stage, 0]
        for index in range(1, len(members) + 1):
            total = total + gram[stage, index]

    sums = jnp.broadcast_to(jnp.sum(total, axis=1, keepdims=True), (16, LANES))
    entry = {}
    for index, (i, j) in enumerate(GRAM):
        entry[i, j] = entry[j, i] = sums[index : index + 1, :]

    def inner(left, right):
        value = None
        for i, u in enumerate(left):
            for j, v in enumerate(right):
                term = u * v * entry[i, j]
                value = term if value is None else value + term
        return value

    one = jnp.ones((1, LANES), jnp.float32)
    residual, direction = [one], [one]
    dipole = []
    rz_value = inner(residual, residual)
    for iteration in range(ITERS):
        size = iteration + 1
        image = [
            (direction[k] if k < size else 0.0) - (direction[k - 1] if k > 0 else 0.0)
            for k in range(size + 1)
        ]
        length = rz_value / inner(direction, image)
        dipole = [
            length * direction[k] + (dipole[k] if k < len(dipole) else 0.0) for k in range(size)
        ]
        residual = [
            (residual[k] if k < size else 0.0) - length * image[k] for k in range(size + 1)
        ]
        if iteration + 1 < ITERS:
            rz_next = inner(residual, residual)
            ratio = rz_next / rz_value
            direction = [
                residual[k] + (ratio * direction[k] if k < size else 0.0) for k in range(size + 1)
            ]
            rz_value = rz_next

    for a in range(2):
        moved = direct[a]
        for k in range(ITERS):
            moved = moved + dipole[k] * field[k, a]
        moved = moved * alpha[a]
        left = residual[0] * field[0, a]
        for k in range(1, ITERS + 1):
            left = left + residual[k] * field[k, a]
        for k in range(3):
            for c in range(2):
                lanes = slice(a * BLK + c * LANES, a * BLK + (c + 1) * LANES)
                dip_ref[k : k + 1, lanes] = moved[2 * k + c : 2 * k + c + 1, :]
                res_ref[k : k + 1, lanes] = left[2 * k + c : 2 * k + c + 1, :]


def on_device(spaces, pairs, span_y, positions, polarizability, charges, groups, pair_list, tile_count):
    atoms = positions.shape[1]
    row = lax.axis_index("space")
    slot, partner = pair_list[0, :, 0], pair_list[0, :, 1]
    row_step = partner // BPD - row
    col_step = (partner % BPD - slot + (BPD + 1)) % BPD - 1
    kind = jnp.where(row_step == 0, col_step, row_step * 3 + col_step)
    listed = jnp.arange(pair_list.shape[1]) < tile_count[0]
    key = jnp.where(listed, kind * BPD + slot, -1)
    wanted = jnp.arange(8 * BPD)
    flags = jnp.max((key[:, None] == wanted[None, :]).astype(jnp.float32), axis=0)
    flags = jnp.broadcast_to(flags.reshape(8, BPD, 1), (8, BPD, BLK)).reshape(8, atoms)
    attrs = jnp.concatenate(
        [
            positions,
            polarizability[None],
            charges[None],
            groups.astype(jnp.float32)[None],
            lax.rsqrt(polarizability)[None],
            jnp.zeros((1, atoms), jnp.float32),
            flags,
        ],
        0,
    )
    copies = len(AHEAD) + SWEEPS * len(HALO) + 2 * pairs + span_y + spaces // (2 * span_y) - 3
    share = jax.ShapeDtypeStruct((3, 2 * BLK), jnp.float32)
    vmem = pl.BlockSpec(memory_space=pltpu.VMEM)
    return pl.pallas_call(
        functools.partial(kernel, spaces, pairs, span_y),
        out_shape=(share, share),
        in_specs=[vmem],
        out_specs=(vmem, vmem),
        scratch_shapes=[
            pltpu.VMEM((5, 16, 4 * BLK), jnp.float32),
            pltpu.VMEM((2, 5, BLK, LANES), jnp.float32),
            pltpu.VMEM((32, LANES), jnp.float32),
            pltpu.VMEM((60, 4, BLK, LANES), jnp.float32),
            pltpu.VMEM((2, 3, BLK, LANES), jnp.float32),
            pltpu.VMEM((2, 8, LANES), jnp.float32),
            pltpu.VMEM((2, 8, LANES), jnp.float32),
            pltpu.VMEM((SWEEPS + 1, 5, 4, 8, LANES), jnp.float32),
            pltpu.VMEM((SWEEPS, 2, 8, LANES), jnp.float32),
            pltpu.VMEM((3, 8, 16, LANES), jnp.float32),
            pltpu.SemaphoreType.DMA((copies,)),
            pltpu.SemaphoreType.DMA((copies,)),
        ],
        compiler_params=pltpu.CompilerParams(
            collective_id=0, has_side_effects=True, vmem_limit_bytes=52 * 2**20
        ),
    )(attrs)


def solution(mesh):
    spaces, pairs = mesh.shape["space"], mesh.shape["pair"]
    span_y = 8 if spaces >= 128 else 2
    return jax.shard_map(
        functools.partial(on_device, spaces, pairs, span_y),
        mesh=mesh,
        in_specs=(
            P(None, "space"),
            P("space"),
            P("space"),
            P("space"),
            P("space", None, None),
            P("space"),
        ),
        out_specs=(P(None, ("space", "pair")), P(None, ("space", "pair"))),
        check_vma=False,
    )
```

time: 1360 us -> 89.9 us (0.07)
  blocking collectives: 525 us -> 0 us
  loops' own time: 360 us -> 0 us
  waiting for transfers between devices: 162 us -> 0 us
  other arithmetic: 142 us -> 0.12 us
  Pallas kernels: 0 us -> 83.8 us
  starting transfers between devices: 70.5 us -> 0 us
  local copies, waits for them, and re-layouts: 71.8 us -> 4.02 us
  between operations: 21.7 us -> 1.32 us
    psum x5 -> x0, blocking collectives: 488 us -> none  [the longest x3 290 us: precond_sum(): return lax.psum(jnp.sum(first_vec * second_vec), ('space', 'pair'))]
    another operation x5 -> x0, loops' own time: 360 us -> none  [sweep(): return lax.fori_loop(0, visits, visit, zeroed)]
    unnamed x10 -> x0, waiting for transfers between devices: 138 us -> none
    pallas_call x0 -> x1, Pallas kernels: none -> 83.8 us  [on_device(): pl.pallas_call(functools.partial(kernel, spaces, pairs, span_y), out_shap...]
    reduce_sum x229 -> x0, other arithmetic: 70.6 us -> none  [the longest x64 27.1 us: dipole_pair(): along_i = jnp.sum(displacement * dipole_i[:, :, None], 0)]
    ppermute x20 -> x0, starting transfers between devices: 70.3 us -> none  [shifted(): lax.ppermute(value, axis, [(source, source + steps) for source in range(f...]
    mul x226 -> x0, other arithmetic: 61.1 us -> none  [the longest x64 28.8 us: dipole_pair(): coef_five * along_j]
    dynamic_slice x81 -> x0, local copies, waits for them, and re-layouts: 52.1 us -> none  [the longest x80 52.1 us: visit(): partner = pair_list[0, tile_row, 1]]
  transfers between devices with their start and end apart: 25 -> 0, of which waited for: 19 -> 0; matrix products, arithmetic and copies ran while one was open for 0% -> 0% of each run, Pallas kernels for 0% -> 0%
where the time goes in v1:
time: 89.9 us; the launch traced here: 89.3 us
  Pallas kernels  83.8 us (93%)
  local copies, waits for them, and re-layouts  4.02 us (4%)
  between operations  1.32 us (1%)
    pallas_call x1, Pallas kernels, on_device(): pl.pallas_call(functools.partial(kernel, spaces, pairs, span_y), out_shap...  83.8 us
    unnamed x12, local copies, waits for them, and re-layouts  3.7 us

profile of v1, /device:TPU:1, one launch (start us, length us, event | category | flops | bytes accessed | tf_op | source)
XLA Modules:
  0.0 89.3 jit_solution(17592864008963341784)
XLA Ops:
  1.3 0.0 copy-start.4
  1.3 0.7 copy-done.4
  2.0 0.0 copy-start.3
  2.0 0.1 convert_reduce_fusion
  2.1 0.1 broadcast_in_dim.31
  2.2 0.1 copy.9
  2.2 0.4 copy-done.3
  2.7 0.0 copy-start.1
  2.7 0.7 copy-done.1
  3.4 0.0 copy-start
  3.4 0.1 broadcast_in_dim.32
  3.5 0.0 copy-start.2
  3.5 0.7 copy-done
  4.1 0.0 copy-done.2
  4.2 0.1 concatenate.3.attr_ref
  4.3 83.8 %shard_map.77 = (f32[3,512]{1,0:T(4,128)S(1)}, f32[3,512]{1,0:T(4,128)S(1)}) custom-call(f32[16,2048]{1,0:T(8,128)S(1)} %concatenate.3.attr_ref), custom_call_target="tpu_custom_call" | custom-call | tf_op jit(solution)/shard_map/pallas_call | solution.py:422
  88.1 0.6 copy.13
  88.7 0.6 copy.14
  (4 shorter events, 0.0 us)
Async XLA Ops:
  1.3 0.7 copy-start.4
  2.0 0.7 copy-start.3
  2.7 0.7 copy-start.1
  3.4 0.8 copy-start
  3.5 0.7 copy-start.2

commit v2 on v1

v2 whole, which is shorter than its diff:
```python
import functools

import jax
import jax.numpy as jnp
from jax import lax
from jax.experimental import pallas as pl
from jax.experimental.pallas import tpu as pltpu
from jax.sharding import PartitionSpec as P

BLK = 256
BPD = 8
ITERS = 3
LANES = 128
SUBS = 8
TILES = BLK // SUBS
BUILD = 4
APPLY = 8
PERIOD = BPD * 8 * 2.15
THOLE = 0.39
SWEEPS = ITERS + 1
MESH = pl.DeviceIdType.MESH

NEAR = [-2, -1, 1, 2]
REACH = [-2, 2, -1, 1, 0]
TARGETS = {1: (0, 0, NEAR), 3: (0, -1, REACH), 2: (1, 0, NEAR), 0: (1, 1, REACH)}
HALO = [(column, d) for column in (1, 3, 2, 0) for d in TARGETS[column][2]]
X, Y, Z, GROUP, ROOT, CHARGE = range(6)
GRAM = [(i, j) for i in range(ITERS) for j in range(i, ITERS + 1)]


def kernel(
    spaces,
    pairs,
    span_y,
    positions_ref,
    polar_ref,
    charges_ref,
    groups_ref,
    list_ref,
    count_ref,
    dip_ref,
    res_ref,
    positions,
    polar,
    charges,
    groups,
    listing,
    flags,
    window,
    wide,
    column,
    weight,
    coef,
    acc,
    alpha,
    direct,
    vec,
    spread,
    field,
    gram,
    load_sem,
    send_sem,
    recv_sem,
):
    loads = [
        pltpu.make_async_copy(source, target, load_sem.at[index])
        for index, (source, target) in enumerate(
            (
                (positions_ref, positions),
                (polar_ref, polar),
                (charges_ref, charges),
                (groups_ref, groups),
                (list_ref, listing),
            )
        )
    ]
    for load in loads:
        load.start()

    sp = lax.axis_index("space")
    pr = lax.axis_index("pair")
    core = lax.rem(sp, 2)
    y = lax.rem(sp // 2, span_y)
    z = sp // (2 * span_y)
    span_z = spaces // (2 * span_y)

    def at_space(d):
        return lax.rem(sp + (d + spaces), spaces)

    def at_pair(e):
        return lax.rem(pr + (e + pairs), pairs)

    def at_core(c):
        return sp - core + lax.rem(core + c, 2)

    stages = [
        (
            [(at_core(c), at_pair(k)) for k in range(pairs) for c in range(2) if (k, c) != (0, 0)],
            pr * 2 + core,
        ),
        (
            [(sp + (lax.rem(y + k, span_y) - y) * 2, pr) for k in range(1, span_y)],
            y,
        ),
        (
            [(sp + (lax.rem(z + k, span_z) - z) * 2 * span_y, pr) for k in range(1, span_z)],
            z,
        ),
    ]

    barrier = pltpu.get_barrier_semaphore()
    partners = [(at_space(d), at_pair(e)) for d in REACH for e in (-1, 0, 1) if (d, e) != (0, 0)]
    for members, _ in stages:
        partners = partners + members
    for partner in partners:
        pl.semaphore_signal(barrier, inc=1, device_id=partner, device_id_type=MESH)

    for load in loads:
        load.wait()

    slot, partner = listing[0:1, :], listing[1:2, :]
    row_step = partner // BPD - sp
    col_step = (partner % BPD - slot + (BPD + 1)) % BPD - 1
    kind = jnp.where(row_step == 0, col_step, row_step * 3 + col_step)
    entry = lax.broadcasted_iota(jnp.int32, slot.shape, 1)
    key = jnp.where(entry < count_ref[0], kind * BPD + slot, -1)
    wanted = lax.broadcasted_iota(jnp.int32, (32, slot.shape[1]), 0)
    wanted = (wanted // 4) * BPD + (2 * pr + (BPD - 1) + wanted % 4) % BPD
    found = jnp.max((key == wanted).astype(jnp.float32), axis=1, keepdims=True)
    flags[...] = jnp.broadcast_to(found, (32, LANES))

    low = jnp.where(pr == 0, -PERIOD, 0.0).astype(jnp.float32)
    high = jnp.where(pr == pairs - 1, PERIOD, 0.0).astype(jnp.float32)
    for k in range(4):
        block = lax.rem(2 * pr + (k - 1 + BPD), BPD)
        for c in range(2):
            lanes = pl.ds(pl.multiple_of(block * BLK + c * LANES, LANES), LANES)
            shift = {0: low, 3: high}.get(k, 0.0)
            lines = {
                X: positions[0:1, lanes] + shift,
                Y: positions[1:2, lanes],
                Z: positions[2:3, lanes],
                GROUP: groups[0:1, lanes].astype(jnp.float32),
                ROOT: lax.rsqrt(polar[0:1, lanes]),
                CHARGE: charges[0:1, lanes],
            }
            for line, value in lines.items():
                window[2, k, c, line : line + 1, :] = value
            window[2, k, c, 6:8, :] = jnp.zeros((2, LANES), jnp.float32)
            if k in (1, 2):
                for m in range(3):
                    alpha[k - 1, 2 * m + c : 2 * m + c + 1, :] = polar[0:1, lanes]
        for m in range(8):
            window[2, k, 2, m : m + 1, :] = flags[4 * m + k : 4 * m + k + 1, :]

    for a in range(2):
        for c in range(2):
            turned = window[2, a + 1, c].T
            for k in (X, Y, Z, GROUP, ROOT):
                values = jnp.broadcast_to(turned[:, k : k + 1], (LANES, LANES))
                if k == ROOT:
                    values = values * THOLE
                half = LANES // SUBS
                column[a, k, c * half : (c + 1) * half] = values.reshape(half, SUBS, LANES)
        alpha[a, 6:8, :] = jnp.zeros((2, LANES), jnp.float32)

    def widen(row, col):
        for c in range(2):
            for k in range(6):
                line = window[row, col, c, k : k + 1, :]
                wide[row, col, c, k] = jnp.broadcast_to(line, (SUBS, LANES))

    def widen_own(col, carry):
        widen(2, col)
        return carry

    def widen_rest(index, carry):
        row = index // 4
        widen(row + row // 2, index % 4)
        return carry

    pl.semaphore_wait(barrier, len(partners))

    def attr_copy(index, d):
        return pltpu.make_async_remote_copy(
            src_ref=window.at[2],
            dst_ref=window.at[2 - d],
            send_sem=send_sem.at[index],
            recv_sem=recv_sem.at[index],
            device_id=(at_space(d), pr),
            device_id_type=MESH,
        )

    for index, d in enumerate(NEAR):
        attr_copy(index, d).start()

    def weigh(a, row, step):
        slot = a * 15 + row * 3 + step
        dx = step - 1
        if row == 2:
            entry, col = (abs(dx), a + step if dx < 0 else a + 1)
        elif row > 2:
            entry, col = ((2, 5)[row - 3] + dx + 1, a + 1)
        else:
            entry, col = ((5, 2)[row] - dx + 1, a + step)
        line = window[min(row, 2), col, 2, entry : entry + 1, :]
        weight[slot] = jnp.broadcast_to(line, (SUBS, LANES))

    def build(a, part, row, step, c, totals, itself):
        def far(line):
            return wide[row, a + step, c, line]

        rx = column[a, X, part] - far(X)
        ry = column[a, Y, part] - far(Y)
        rz = column[a, Z, part] - far(Z)
        squared = jnp.maximum(rx * rx + ry * ry + rz * rz, 1.0)
        inverse = lax.rsqrt(squared)
        inverse_sq = inverse * inverse
        damping = (squared * (squared * inverse)) * (column[a, ROOT, part] * far(ROOT))
        decayed = jnp.exp(-damping)
        third = 1.0 - decayed
        fifth = third - damping * decayed
        tile = a * 15 + row * 3 + step
        weighted = (inverse_sq * inverse) * weight[tile]
        three = third * weighted
        five = (fifth * inverse_sq) * (weighted * 3.0)
        root = five * lax.rsqrt(jnp.maximum(five, 1e-30))
        index = tile * 2 + c
        coef[index, 0, part] = rx * root
        coef[index, 1, part] = ry * root
        coef[index, 2, part] = rz * root
        if itself:
            shape = (BUILD, SUBS, LANES)
            own = lax.broadcasted_iota(jnp.int32, shape, 0) * SUBS + part.start * SUBS
            own = own + lax.broadcasted_iota(jnp.int32, shape, 1)
            other = lax.broadcasted_iota(jnp.int32, shape, 2) + c * LANES
            coef[index, 3, part] = jnp.where(own == other, 0.0, three)
        else:
            coef[index, 3, part] = three
        charged = jnp.where(column[a, GROUP, part] != far(GROUP), three * far(CHARGE), 0.0)
        ex, ey, ez = totals
        return (ex + charged * rx, ey + charged * ry, ez + charged * rz)

    def apply(a, part, row, step, c, totals):
        index = (a * 15 + row * 3 + step) * 2 + c
        sx, sy, sz, three = (coef[index, k, part] for k in range(4))
        vx, vy, vz = (spread[row, a + step, 2 * k + c] for k in range(3))
        along = sx * vx + sy * vy + sz * vz
        ex, ey, ez = totals
        return (
            ex + (along * sx - three * vx),
            ey + (along * sy - three * vy),
            ez + (along * sz - three * vz),
        )

    def zeros(size):
        return tuple(jnp.zeros((size, SUBS, LANES), jnp.float32) for _ in range(3))

    def load_acc(a, part):
        return tuple(acc[a, k, part] for k in range(3))

    def store_acc(a, part, totals):
        for k in range(3):
            acc[a, k, part] = totals[k]

    def summed(a):
        parts = []
        for k in range(3):
            for c in range(2):
                half = LANES // SUBS
                turned = acc[a, k, c * half : (c + 1) * half].reshape(LANES, LANES).T
                parts.append(jnp.sum(turned, axis=0, keepdims=True))
        parts.append(jnp.zeros((2, LANES), jnp.float32))
        return jnp.concatenate(parts, axis=0)

    base = len(NEAR)

    def halo_copy(n, index):
        col, d = HALO[index]
        block, e, _ = TARGETS[col]
        number = base + n * len(HALO) + index
        return pltpu.make_async_remote_copy(
            src_ref=vec.at[n, 2, block + 1],
            dst_ref=vec.at[n, 2 - d, col],
            send_sem=send_sem.at[number],
            recv_sem=recv_sem.at[number],
            device_id=(at_space(d), at_pair(e)),
            device_id_type=MESH,
        )

    def send(n, block):
        for index, (col, _) in enumerate(HALO):
            if TARGETS[col][0] == block:
                halo_copy(n, index).start()

    def arrive(n, wanted_col):
        for index, (col, _) in enumerate(HALO):
            if col == wanted_col:
                halo_copy(n, index).wait()

    for a in range(2):
        for step in range(3):
            for row in (2, 3, 4):
                weigh(a, row, step)

    lax.fori_loop(0, 4, widen_own, 0)

    def build_own(group, carry):
        a = group // (TILES // BUILD)
        part = pl.ds((group - a * (TILES // BUILD)) * BUILD, BUILD)
        totals = zeros(BUILD)
        for step in range(3):
            for c in range(2):
                totals = build(a, part, 2, step, c, totals, step == 1)
        store_acc(a, part, totals)
        return carry

    lax.fori_loop(0, 2 * (TILES // BUILD), build_own, 0)
    for index, d in enumerate(NEAR):
        attr_copy(index, d).wait()
    for a in range(2):
        for step in range(3):
            for row in (0, 1):
                weigh(a, row, step)
    lax.fori_loop(0, 16, widen_rest, 0)

    def build_rest(a, carry):
        def one_group(group, inner):
            part = pl.ds(group * BUILD, BUILD)

            def one_row(index, totals):
                row = index + index // 2
                for step in range(3):
                    for c in range(2):
                        totals = build(a, part, row, step, c, totals, False)
                return totals

            store_acc(a, part, lax.fori_loop(0, 4, one_row, load_acc(a, part)))
            return inner

        lax.fori_loop(0, TILES // BUILD, one_group, 0)
        value = summed(a)
        direct[a] = value
        vec[0, 2, a + 1] = value * alpha[a]
        for block in range(2):

            @pl.when(a == block)
            def _():
                send(0, block)

        return carry

    lax.fori_loop(0, 2, build_rest, 0)

    def ready(n, col):
        arrive(n, col)

        def one_row(row, carry):
            for m in range(6):
                line = vec[n, row, col, m : m + 1, :]
                spread[row, col, m] = jnp.broadcast_to(line, (SUBS, LANES))
            return carry

        lax.fori_loop(0, 5, one_row, 0)

    def strips(a, steps, fresh):
        def one_group(group, carry):
            part = pl.ds(group * APPLY, APPLY)
            totals = zeros(APPLY) if fresh else load_acc(a, part)
            for step in steps:
                for row in range(5):
                    for c in range(2):
                        totals = apply(a, part, row, step, c, totals)
            store_acc(a, part, totals)
            return carry

        lax.fori_loop(0, TILES // APPLY, one_group, 0)

    def finish(n, a):
        value = summed(a)
        field[n, a] = value
        vec[n + 1, 2, a + 1] = value * alpha[a]

        @pl.when(n + 1 < SWEEPS)
        def _():
            send(n + 1, a)

    def sweep(n, carry):
        ready(n, 1)
        strips(0, (1,), True)
        strips(1, (0,), True)
        ready(n, 2)
        ready(n, 0)
        strips(0, (0, 2), False)
        finish(n, 0)
        ready(n, 3)
        strips(1, (2, 1), False)
        finish(n, 1)
        return carry

    lax.fori_loop(0, SWEEPS, sweep, 0)

    lines = []
    for i, j in GRAM:
        product = field[i, 0] * (alpha[0] * field[j, 0]) + field[i, 1] * (alpha[1] * field[j, 1])
        lines.append(jnp.sum(product, axis=0, keepdims=True))
    lines.append(jnp.zeros((16 - len(GRAM), LANES), jnp.float32))
    total = jnp.concatenate(lines, axis=0)
    first = base + SWEEPS * len(HALO)
    for stage, (members, mine) in enumerate(stages):
        gram[stage, mine] = total
        copies = []
        for index, member in enumerate(members):
            copies.append(
                pltpu.make_async_remote_copy(
                    src_ref=gram.at[stage, mine],
                    dst_ref=gram.at[stage, mine],
                    send_sem=send_sem.at[first + index],
                    recv_sem=recv_sem.at[first + index],
                    device_id=member,
                    device_id_type=MESH,
                )
            )
            copies[-1].start()
        for copy in copies:
            copy.wait()
        first += len(members)
        total = gram[stage, 0]
        for index in range(1, len(members) + 1):
            total = total + gram[stage, index]

    sums = jnp.broadcast_to(jnp.sum(total, axis=1, keepdims=True), (16, LANES))
    entry = {}
    for index, (i, j) in enumerate(GRAM):
        entry[i, j] = entry[j, i] = sums[index : index + 1, :]

    def inner(left, right):
        value = None
        for i, u in enumerate(left):
            for j, v in enumerate(right):
                term = u * v * entry[i, j]
                value = term if value is None else value + term
        return value

    one = jnp.ones((1, LANES), jnp.float32)
    residual, direction = [one], [one]
    dipole = []
    rz_value = inner(residual, residual)
    for iteration in range(ITERS):
        size = iteration + 1
        image = [
            (direction[k] if k < size else 0.0) - (direction[k - 1] if k > 0 else 0.0)
            for k in range(size + 1)
        ]
        length = rz_value / inner(direction, image)
        dipole = [
            length * direction[k] + (dipole[k] if k < len(dipole) else 0.0) for k in range(size)
        ]
        residual = [
            (residual[k] if k < size else 0.0) - length * image[k] for k in range(size + 1)
        ]
        if iteration + 1 < ITERS:
            rz_next = inner(residual, residual)
            ratio = rz_next / rz_value
            direction = [
                residual[k] + (ratio * direction[k] if k < size else 0.0) for k in range(size + 1)
            ]
            rz_value = rz_next

    for a in range(2):
        moved = direct[a]
        for k in range(ITERS):
            moved = moved + dipole[k] * field[k, a]
        moved = moved * alpha[a]
        left = residual[0] * field[0, a]
        for k in range(1, ITERS + 1):
            left = left + residual[k] * field[k, a]
        for k in range(3):
            for c in range(2):
                lanes = slice(a * BLK + c * LANES, a * BLK + (c + 1) * LANES)
                dip_ref[k : k + 1, lanes] = moved[2 * k + c : 2 * k + c + 1, :]
                res_ref[k : k + 1, lanes] = left[2 * k + c : 2 * k + c + 1, :]


def on_device(spaces, pairs, span_y, positions, polarizability, charges, groups, pair_list, tile_count):
    atoms = positions.shape[1]
    listed = pair_list.shape[1]
    copies = len(NEAR) + SWEEPS * len(HALO) + 2 * pairs + span_y + spaces // (2 * span_y) - 3
    share = jax.ShapeDtypeStruct((3, 2 * BLK), jnp.float32)
    vmem = pl.BlockSpec(memory_space=pltpu.VMEM)
    hbm = pl.BlockSpec(memory_space=pltpu.HBM)
    return pl.pallas_call(
        functools.partial(kernel, spaces, pairs, span_y),
        out_shape=(share, share),
        in_specs=[hbm] * 5 + [pl.BlockSpec(memory_space=pltpu.SMEM)],
        out_specs=(vmem, vmem),
        scratch_shapes=[
            pltpu.VMEM((3, atoms), jnp.float32),
            pltpu.VMEM((1, atoms), jnp.float32),
            pltpu.VMEM((1, atoms), jnp.float32),
            pltpu.VMEM((1, atoms), jnp.int32),
            pltpu.VMEM((2, listed), jnp.int32),
            pltpu.VMEM((32, LANES), jnp.float32),
            pltpu.VMEM((5, 4, 3, SUBS, LANES), jnp.float32),
            pltpu.VMEM((5, 4, 2, 6, SUBS, LANES), jnp.float32),
            pltpu.VMEM((2, 5, TILES, SUBS, LANES), jnp.float32),
            pltpu.VMEM((30, SUBS, LANES), jnp.float32),
            pltpu.VMEM((60, 4, TILES, SUBS, LANES), jnp.float32),
            pltpu.VMEM((2, 3, TILES, SUBS, LANES), jnp.float32),
            pltpu.VMEM((2, 8, LANES), jnp.float32),
            pltpu.VMEM((2, 8, LANES), jnp.float32),
            pltpu.VMEM((SWEEPS + 1, 5, 4, SUBS, LANES), jnp.float32),
            pltpu.VMEM((5, 4, 6, SUBS, LANES), jnp.float32),
            pltpu.VMEM((SWEEPS, 2, 8, LANES), jnp.float32),
            pltpu.VMEM((3, 8, 16, LANES), jnp.float32),
            pltpu.SemaphoreType.DMA((5,)),
            pltpu.SemaphoreType.DMA((copies,)),
            pltpu.SemaphoreType.DMA((copies,)),
        ],
        compiler_params=pltpu.CompilerParams(
            collective_id=0, has_side_effects=True, vmem_limit_bytes=56 * 2**20
        ),
    )(
        positions,
        polarizability[None],
        charges[None],
        groups[None],
        pair_list[0].T,
        tile_count,
    )


def solution(mesh):
    spaces, pairs = mesh.shape["space"], mesh.shape["pair"]
    span_y = 8 if spaces >= 128 else 2
    return jax.shard_map(
        functools.partial(on_device, spaces, pairs, span_y),
        mesh=mesh,
        in_specs=(
            P(None, "space"),
            P("space"),
            P("space"),
            P("space"),
            P("space", None, None),
            P("space"),
        ),
        out_specs=(P(None, ("space", "pair")), P(None, ("space", "pair"))),
        check_vma=False,
    )
```

time: 89.9 us -> 91.5 us (1.018)
  Pallas kernels: 83.8 us -> 87.8 us
  local copies, waits for them, and re-layouts: 4.02 us -> 1.9 us
    pallas_call x1, Pallas kernels: 83.8 us -> 87.8 us  [on_device(): pl.pallas_call(functools.partial(kernel, spaces, pairs, span_y), out_shap...]
    unnamed x12 -> x4, local copies, waits for them, and re-layouts: 3.7 us -> 1.9 us
where the time goes in v2:
time: 91.5 us; the launch traced here: 91 us
  Pallas kernels  87.8 us (96%)
  local copies, waits for them, and re-layouts  1.9 us (2%)
  between operations  1.29 us (1%)
    pallas_call x1, Pallas kernels, on_device(): pl.pallas_call(functools.partial(kernel, spaces, pairs, span_y), out_shap...  87.8 us
    unnamed x4, local copies, waits for them, and re-layouts  1.9 us

profile of v2, /device:TPU:1, one launch (start us, length us, event | category | flops | bytes accessed | tf_op | source)
XLA Modules:
  0.0 91.0 jit_solution(9188676553982621197)
XLA Ops:
  1.3 87.8 %shard_map.77 = (f32[3,512]{1,0:T(4,128)}, f32[3,512]{1,0:T(4,128)}) custom-call(f32[3,2048]{1,0:T(4,128)} %positions_ref.1, f32[1,2048]{1,0:T(1,128)} %bitcast.6, f32[1,2048]{1,0:T(1,128)} %bitcast.7, s32[1,2048]{1,0:T(1,128)} %bitcast.8, s32[2,64]{1,0:T(2,128)} %bitcast.9, s32[1]{0:T(128)S(6)} %copy.10.count_ref), custom_call_target="tpu_custom_call" | custom-call | tf_op jit(solution)/shard_map/pallas_call | solution.py:492
  89.1 0.0 copy-start
  89.1 1.3 %copy.11 = f32[3,512]{1,0:T(4,128)} copy(f32[3,512]{1,0:T(4,128)} %get-tuple-element.4) | data formatting | bytes 12288
  90.4 0.0 copy-done
  90.4 0.6 copy.12
Async XLA Ops:
  89.1 1.3 %copy-start = (f32[3,512]{1,0:T(4,128)S(1)}, f32[3,512]{1,0:T(4,128)}, u32[]{:S(2)}) copy-start(f32[3,512]{1,0:T(4,128)} %get-tuple-element.5) | copy-start | bytes 18436

commit v3 on v2

--- a/solution.py
+++ b/solution.py
@@ -17,6 +17,7 @@
 APPLY = 8
 PERIOD = BPD * 8 * 2.15
 THOLE = 0.39
+ROOT_THREE = 3.0**0.5
 SWEEPS = ITERS + 1
 MESH = pl.DeviceIdType.MESH
 
@@ -51,11 +52,14 @@
     column,
     weight,
     coef,
+    cubes,
+    cubed,
     acc,
     alpha,
     direct,
     vec,
     spread,
+    pieces,
     field,
     gram,
     load_sem,
@@ -159,7 +163,7 @@
             for k in (X, Y, Z, GROUP, ROOT):
                 values = jnp.broadcast_to(turned[:, k : k + 1], (LANES, LANES))
                 if k == ROOT:
-                    values = values * THOLE
+                    values = values * -THOLE
                 half = LANES // SUBS
                 column[a, k, c * half : (c + 1) * half] = values.reshape(half, SUBS, LANES)
         alpha[a, 6:8, :] = jnp.zeros((2, LANES), jnp.float32)
@@ -204,27 +208,28 @@
         else:
             entry, col = ((5, 2)[row] - dx + 1, a + step)
         line = window[min(row, 2), col, 2, entry : entry + 1, :]
-        weight[slot] = jnp.broadcast_to(line, (SUBS, LANES))
-
-    def build(a, part, row, step, c, totals, itself):
+        weight[slot, 0] = jnp.broadcast_to(line, (SUBS, LANES))
+        weight[slot, 1] = jnp.broadcast_to(line * ROOT_THREE, (SUBS, LANES))
+
+    def build(a, part, row, step, c, totals, itself, masked):
         def far(line):
             return wide[row, a + step, c, line]
 
         rx = column[a, X, part] - far(X)
         ry = column[a, Y, part] - far(Y)
         rz = column[a, Z, part] - far(Z)
-        squared = jnp.maximum(rx * rx + ry * ry + rz * rz, 1.0)
+        squared = rx * rx + ry * ry + rz * rz
+        if itself:
+            squared = jnp.maximum(squared, 1.0)
         inverse = lax.rsqrt(squared)
         inverse_sq = inverse * inverse
         damping = (squared * (squared * inverse)) * (column[a, ROOT, part] * far(ROOT))
-        decayed = jnp.exp(-damping)
+        decayed = jnp.exp(damping)
         third = 1.0 - decayed
-        fifth = third - damping * decayed
+        fifth = (third + damping * decayed) * inverse
         tile = a * 15 + row * 3 + step
-        weighted = (inverse_sq * inverse) * weight[tile]
-        three = third * weighted
-        five = (fifth * inverse_sq) * (weighted * 3.0)
-        root = five * lax.rsqrt(jnp.maximum(five, 1e-30))
+        three = (third * (inverse_sq * inverse)) * weight[tile, 0]
+        root = (fifth * lax.rsqrt(fifth)) * (inverse_sq * weight[tile, 1])
         index = tile * 2 + c
         coef[index, 0, part] = rx * root
         coef[index, 1, part] = ry * root
@@ -234,24 +239,28 @@
             own = lax.broadcasted_iota(jnp.int32, shape, 0) * SUBS + part.start * SUBS
             own = own + lax.broadcasted_iota(jnp.int32, shape, 1)
             other = lax.broadcasted_iota(jnp.int32, shape, 2) + c * LANES
-            coef[index, 3, part] = jnp.where(own == other, 0.0, three)
-        else:
-            coef[index, 3, part] = three
-        charged = jnp.where(column[a, GROUP, part] != far(GROUP), three * far(CHARGE), 0.0)
+            three = jnp.where(own == other, 0.0, three)
+        flat = three.reshape(BUILD * SUBS, LANES)
+        high = flat.astype(jnp.bfloat16)
+        low = (flat - high.astype(jnp.float32)).astype(jnp.bfloat16)
+        first = pl.multiple_of(part.start * SUBS, BUILD * SUBS)
+        rows = pl.ds(first, BUILD * SUBS)
+        lanes = pl.ds(pl.multiple_of((step * 5 + row) * LANES, LANES), LANES)
+        cubes[a, 2 * c, rows, lanes] = high
+        cubes[a, 2 * c + 1, rows, lanes] = low
+        charged = three * far(CHARGE)
+        if masked:
+            charged = jnp.where(column[a, GROUP, part] != far(GROUP), charged, 0.0)
         ex, ey, ez = totals
         return (ex + charged * rx, ey + charged * ry, ez + charged * rz)
 
     def apply(a, part, row, step, c, totals):
         index = (a * 15 + row * 3 + step) * 2 + c
-        sx, sy, sz, three = (coef[index, k, part] for k in range(4))
+        sx, sy, sz = (coef[index, k, part] for k in range(3))
         vx, vy, vz = (spread[row, a + step, 2 * k + c] for k in range(3))
         along = sx * vx + sy * vy + sz * vz
         ex, ey, ez = totals
-        return (
-            ex + (along * sx - three * vx),
-            ey + (along * sy - three * vy),
-            ez + (along * sz - three * vz),
-        )
+        return (ex + along * sx, ey + along * sy, ez + along * sz)
 
     def zeros(size):
         return tuple(jnp.zeros((size, SUBS, LANES), jnp.float32) for _ in range(3))
@@ -263,13 +272,23 @@
         for k in range(3):
             acc[a, k, part] = totals[k]
 
-    def summed(a):
+    def summed(a, with_cubes):
+        if with_cubes:
+            less = [
+                cubed[a, c, 0:8] + cubed[a, c, 8:16] + cubed[a, c, 16:24] for c in range(2)
+            ]
         parts = []
         for k in range(3):
             for c in range(2):
                 half = LANES // SUBS
                 turned = acc[a, k, c * half : (c + 1) * half].reshape(LANES, LANES).T
-                parts.append(jnp.sum(turned, axis=0, keepdims=True))
+                part = jnp.sum(turned, axis=0, keepdims=True)
+                if with_cubes:
+                    lanes = slice(c * LANES, (c + 1) * LANES)
+                    part = part - (
+                        less[0][2 * k : 2 * k + 1, lanes] + less[1][2 * k + 1 : 2 * k + 2, lanes]
+                    )
+                parts.append(part)
         parts.append(jnp.zeros((2, LANES), jnp.float32))
         return jnp.concatenate(parts, axis=0)
 
@@ -311,7 +330,7 @@
         totals = zeros(BUILD)
         for step in range(3):
             for c in range(2):
-                totals = build(a, part, 2, step, c, totals, step == 1)
+                totals = build(a, part, 2, step, c, totals, step == 1, True)
         store_acc(a, part, totals)
         return carry
 
@@ -328,18 +347,22 @@
         def one_group(group, inner):
             part = pl.ds(group * BUILD, BUILD)
 
-            def one_row(index, totals):
-                row = index + index // 2
+            def one_row(row, totals, masked):
                 for step in range(3):
                     for c in range(2):
-                        totals = build(a, part, row, step, c, totals, False)
+                        totals = build(
+                            a, part, row, step, c, totals, False, step == masked
+                        )
                 return totals
 
-            store_acc(a, part, lax.fori_loop(0, 4, one_row, load_acc(a, part)))
+            totals = load_acc(a, part)
+            totals = lax.fori_loop(0, 2, functools.partial(one_row, masked=0), totals)
+            totals = lax.fori_loop(3, 5, functools.partial(one_row, masked=2), totals)
+            store_acc(a, part, totals)
             return inner
 
         lax.fori_loop(0, TILES // BUILD, one_group, 0)
-        value = summed(a)
+        value = summed(a, False)
         direct[a] = value
         vec[0, 2, a + 1] = value * alpha[a]
         for block in range(2):
@@ -356,28 +379,51 @@
         arrive(n, col)
 
         def one_row(row, carry):
+            tile = vec[n, row, col]
             for m in range(6):
-                line = vec[n, row, col, m : m + 1, :]
-                spread[row, col, m] = jnp.broadcast_to(line, (SUBS, LANES))
+                spread[row, col, m] = jnp.broadcast_to(tile[m : m + 1, :], (SUBS, LANES))
+            high = tile.astype(jnp.bfloat16).astype(jnp.float32)
+            rest = tile - high
+            middle = rest.astype(jnp.bfloat16).astype(jnp.float32)
+            low = rest - middle
+            parts = jnp.concatenate([high, middle, low, jnp.zeros_like(low)], axis=0)
+            lanes = pl.ds(pl.multiple_of((col * 5 + row) * LANES, LANES), LANES)
+            pieces[:, lanes] = parts.astype(jnp.bfloat16)
             return carry
 
         lax.fori_loop(0, 5, one_row, 0)
 
     def strips(a, steps, fresh):
+        if fresh:
+            cubed[a] = jnp.zeros((2, 4 * SUBS, BLK), jnp.float32)
+
         def one_group(group, carry):
             part = pl.ds(group * APPLY, APPLY)
+            c = group // 2
+            product = None
+            for step in steps:
+                own = pieces[:, (a + step) * 5 * LANES : (a + step + 1) * 5 * LANES]
+                other = cubes[a, group, :, step * 5 * LANES : (step + 1) * 5 * LANES]
+                term = lax.dot_general(
+                    own,
+                    other,
+                    (((1,), (1,)), ((), ())),
+                    preferred_element_type=jnp.float32,
+                )
+                product = term if product is None else product + term
             totals = zeros(APPLY) if fresh else load_acc(a, part)
             for step in steps:
                 for row in range(5):
-                    for c in range(2):
-                        totals = apply(a, part, row, step, c, totals)
+                    for k in range(2):
+                        totals = apply(a, part, row, step, k, totals)
             store_acc(a, part, totals)
+            cubed[a, c] = cubed[a, c] + product
             return carry
 
         lax.fori_loop(0, TILES // APPLY, one_group, 0)
 
     def finish(n, a):
-        value = summed(a)
+        value = summed(a, True)
         field[n, a] = value
         vec[n + 1, 2, a + 1] = value * alpha[a]
 
@@ -504,13 +550,16 @@
             pltpu.VMEM((5, 4, 3, SUBS, LANES), jnp.float32),
             pltpu.VMEM((5, 4, 2, 6, SUBS, LANES), jnp.float32),
             pltpu.VMEM((2, 5, TILES, SUBS, LANES), jnp.float32),
-            pltpu.VMEM((30, SUBS, LANES), jnp.float32),
-            pltpu.VMEM((60, 4, TILES, SUBS, LANES), jnp.float32),
+            pltpu.VMEM((30, 2, SUBS, LANES), jnp.float32),
+            pltpu.VMEM((60, 3, TILES, SUBS, LANES), jnp.float32),
+            pltpu.VMEM((2, 4, BLK, 15 * LANES), jnp.bfloat16),
+            pltpu.VMEM((2, 2, 4 * SUBS, BLK), jnp.float32),
             pltpu.VMEM((2, 3, TILES, SUBS, LANES), jnp.float32),
             pltpu.VMEM((2, 8, LANES), jnp.float32),
             pltpu.VMEM((2, 8, LANES), jnp.float32),
             pltpu.VMEM((SWEEPS + 1, 5, 4, SUBS, LANES), jnp.float32),
             pltpu.VMEM((5, 4, 6, SUBS, LANES), jnp.float32),
+            pltpu.VMEM((4 * SUBS, 20 * LANES), jnp.bfloat16),
             pltpu.VMEM((SWEEPS, 2, 8, LANES), jnp.float32),
             pltpu.VMEM((3, 8, 16, LANES), jnp.float32),
             pltpu.SemaphoreType.DMA((5,)),
@@ -518,14 +567,19 @@
             pltpu.SemaphoreType.DMA((copies,)),
         ],
         compiler_params=pltpu.CompilerParams(
-            collective_id=0, has_side_effects=True, vmem_limit_bytes=56 * 2**20
+            collective_id=0, has_side_effects=True, vmem_limit_bytes=52 * 2**20
         ),
     )(
-        positions,
-        polarizability[None],
-        charges[None],
-        groups[None],
-        pair_list[0].T,
+        *[
+            pltpu.with_memory_space_constraint(value, pltpu.HBM)
+            for value in (
+                positions,
+                polarizability[None],
+                charges[None],
+                groups[None],
+                pair_list[0].T,
+            )
+        ],
         tile_count,
     )
 

time: 91.5 us -> 82.9 us (0.906)
  Pallas kernels: 87.8 us -> 79.8 us
    pallas_call x1, Pallas kernels: 87.8 us -> 79.8 us  [on_device(): pl.pallas_call(functools.partial(kernel, spaces, pairs, span_y), out_shap...]
    unnamed x4 -> x2, local copies, waits for them, and re-layouts: 1.9 us -> 1.2 us
where the time goes in v3:
time: 82.9 us; the launch traced here: 82.3 us
  Pallas kernels  79.8 us (96%)
  between operations  1.29 us (2%)
  local copies, waits for them, and re-layouts  1.2 us (1%)
    pallas_call x1, Pallas kernels, on_device(): pl.pallas_call(functools.partial(kernel, spaces, pairs, span_y), out_shap...  79.8 us

profile of v3, /device:TPU:1, one launch (start us, length us, event | category | flops | bytes accessed | tf_op | source)
XLA Modules:
  0.0 82.3 jit_solution(14797113678479104292)
XLA Ops:
  1.3 79.8 %shard_map.77 = (f32[3,512]{1,0:T(4,128)S(1)}, f32[3,512]{1,0:T(4,128)S(1)}) custom-call(f32[3,2048]{1,0:T(4,128)} %positions_ref.1, f32[1,2048]{1,0:T(1,128)} %bitcast.6, f32[1,2048]{1,0:T(1,128)} %bitcast.7, s32[1,2048]{1,0:T(1,128)} %bitcast.8, s32[2,64]{1,0:T(2,128)} %bitcast.9, s32[1]{0:T(128)S(6)} %copy.10.count_ref), custom_call_target="tpu_custom_call" | custom-call | tf_op jit(solution)/shard_map/pallas_call | solution.py:538
  81.1 0.6 copy.11
  81.7 0.6 copy.12

commit v4 on v3

--- a/solution.py
+++ b/solution.py
@@ -26,6 +26,8 @@
 TARGETS = {1: (0, 0, NEAR), 3: (0, -1, REACH), 2: (1, 0, NEAR), 0: (1, 1, REACH)}
 HALO = [(column, d) for column in (1, 3, 2, 0) for d in TARGETS[column][2]]
 X, Y, Z, GROUP, ROOT, CHARGE = range(6)
+OTHERS = (0, 1, 3, 4)
+EVERY = OTHERS + (2,)
 GRAM = [(i, j) for i in range(ITERS) for j in range(i, ITERS + 1)]
 
 
@@ -168,6 +170,11 @@
                 column[a, k, c * half : (c + 1) * half] = values.reshape(half, SUBS, LANES)
         alpha[a, 6:8, :] = jnp.zeros((2, LANES), jnp.float32)
 
+    def place(row):
+        if isinstance(row, int) and row == 2:
+            return 4
+        return row - row // 3 if isinstance(row, int) else row - lax.div(row, 3)
+
     def widen(row, col):
         for c in range(2):
             for k in range(6):
@@ -245,7 +252,7 @@
         low = (flat - high.astype(jnp.float32)).astype(jnp.bfloat16)
         first = pl.multiple_of(part.start * SUBS, BUILD * SUBS)
         rows = pl.ds(first, BUILD * SUBS)
-        lanes = pl.ds(pl.multiple_of((step * 5 + row) * LANES, LANES), LANES)
+        lanes = pl.ds(pl.multiple_of((step * 5 + place(row)) * LANES, LANES), LANES)
         cubes[a, 2 * c, rows, lanes] = high
         cubes[a, 2 * c + 1, rows, lanes] = low
         charged = three * far(CHARGE)
@@ -312,11 +319,6 @@
             if TARGETS[col][0] == block:
                 halo_copy(n, index).start()
 
-    def arrive(n, wanted_col):
-        for index, (col, _) in enumerate(HALO):
-            if col == wanted_col:
-                halo_copy(n, index).wait()
-
     for a in range(2):
         for step in range(3):
             for row in (2, 3, 4):
@@ -375,25 +377,26 @@
 
     lax.fori_loop(0, 2, build_rest, 0)
 
+    def take(n, row, col):
+        tile = vec[n, row, col]
+        for m in range(6):
+            spread[row, col, m] = jnp.broadcast_to(tile[m : m + 1, :], (SUBS, LANES))
+        high = tile.astype(jnp.bfloat16).astype(jnp.float32)
+        rest = tile - high
+        middle = rest.astype(jnp.bfloat16).astype(jnp.float32)
+        low = rest - middle
+        parts = jnp.concatenate([high, middle, low, jnp.zeros_like(low)], axis=0)
+        lanes = pl.ds((col * 5 + place(row)) * LANES, LANES)
+        pieces[:, lanes] = parts.astype(jnp.bfloat16)
+
     def ready(n, col):
-        arrive(n, col)
-
-        def one_row(row, carry):
-            tile = vec[n, row, col]
-            for m in range(6):
-                spread[row, col, m] = jnp.broadcast_to(tile[m : m + 1, :], (SUBS, LANES))
-            high = tile.astype(jnp.bfloat16).astype(jnp.float32)
-            rest = tile - high
-            middle = rest.astype(jnp.bfloat16).astype(jnp.float32)
-            low = rest - middle
-            parts = jnp.concatenate([high, middle, low, jnp.zeros_like(low)], axis=0)
-            lanes = pl.ds(pl.multiple_of((col * 5 + row) * LANES, LANES), LANES)
-            pieces[:, lanes] = parts.astype(jnp.bfloat16)
-            return carry
-
-        lax.fori_loop(0, 5, one_row, 0)
-
-    def strips(a, steps, fresh):
+        for index, (far, d) in enumerate(HALO):
+            if far == col:
+                halo_copy(n, index).wait()
+                take(n, 2 - d, col)
+
+    def strips(a, steps, rows, fresh):
+        first, last = (place(rows[0]), place(rows[-1]) + 1)
         if fresh:
             cubed[a] = jnp.zeros((2, 4 * SUBS, BLK), jnp.float32)
 
@@ -402,18 +405,19 @@
             c = group // 2
             product = None
             for step in steps:
-                own = pieces[:, (a + step) * 5 * LANES : (a + step + 1) * 5 * LANES]
-                other = cubes[a, group, :, step * 5 * LANES : (step + 1) * 5 * LANES]
+                own = (a + step) * 5
                 term = lax.dot_general(
-                    own,
-                    other,
+                    pieces[:, (own + first) * LANES : (own + last) * LANES],
+                    cubes[
+                        a, group, :, (step * 5 + first) * LANES : (step * 5 + last) * LANES
+                    ],
                     (((1,), (1,)), ((), ())),
                     preferred_element_type=jnp.float32,
                 )
                 product = term if product is None else product + term
             totals = zeros(APPLY) if fresh else load_acc(a, part)
             for step in steps:
-                for row in range(5):
+                for row in rows:
                     for k in range(2):
                         totals = apply(a, part, row, step, k, totals)
             store_acc(a, part, totals)
@@ -432,15 +436,21 @@
             send(n + 1, a)
 
     def sweep(n, carry):
+        take(n, 2, 1)
+        take(n, 2, 2)
+        strips(0, (1, 2), (2,), True)
+        strips(1, (0, 1), (2,), True)
         ready(n, 1)
-        strips(0, (1,), True)
-        strips(1, (0,), True)
+        strips(0, (1,), OTHERS, False)
+        strips(1, (0,), OTHERS, False)
         ready(n, 2)
+        strips(1, (1,), OTHERS, False)
+        strips(0, (2,), OTHERS, False)
         ready(n, 0)
-        strips(0, (0, 2), False)
+        strips(0, (0,), EVERY, False)
         finish(n, 0)
         ready(n, 3)
-        strips(1, (2, 1), False)
+        strips(1, (2,), EVERY, False)
         finish(n, 1)
         return carry
 

time: 82.9 us -> 82.1 us (level)
  Pallas kernels: 79.8 us -> 78.9 us
    pallas_call x1, Pallas kernels: 79.8 us -> 78.9 us  [on_device(): pl.pallas_call(functools.partial(kernel, spaces, pairs, span_y), out_shap...]
where the time goes in v4:
time: 82.1 us; the launch traced here: 81.4 us
  Pallas kernels  78.9 us (96%)
  between operations  1.29 us (2%)
  local copies, waits for them, and re-layouts  1.2 us (1%)
    pallas_call x1, Pallas kernels, on_device(): pl.pallas_call(functools.partial(kernel, spaces, pairs, span_y), out_shap...  78.9 us

profile of v4, /device:TPU:1, one launch (start us, length us, event | category | flops | bytes accessed | tf_op | source)
XLA Modules:
  0.0 81.4 jit_solution(3424926672848583947)
XLA Ops:
  1.3 78.9 %shard_map.77 = (f32[3,512]{1,0:T(4,128)S(1)}, f32[3,512]{1,0:T(4,128)S(1)}) custom-call(f32[3,2048]{1,0:T(4,128)} %positions_ref.1, f32[1,2048]{1,0:T(1,128)} %bitcast.6, f32[1,2048]{1,0:T(1,128)} %bitcast.7, s32[1,2048]{1,0:T(1,128)} %bitcast.8, s32[2,64]{1,0:T(2,128)} %bitcast.9, s32[1]{0:T(128)S(6)} %copy.10.count_ref), custom_call_target="tpu_custom_call" | custom-call | tf_op jit(solution)/shard_map/pallas_call | solution.py:548
  80.2 0.6 copy.11
  80.8 0.6 copy.12

commit v5 on v4

--- a/solution.py
+++ b/solution.py
@@ -28,6 +28,7 @@
 X, Y, Z, GROUP, ROOT, CHARGE = range(6)
 OTHERS = (0, 1, 3, 4)
 EVERY = OTHERS + (2,)
+DISTANT = (0, 4)
 GRAM = [(i, j) for i in range(ITERS) for j in range(i, ITERS + 1)]
 
 
@@ -56,6 +57,11 @@
     coef,
     cubes,
     cubed,
+    fives,
+    fived,
+    apart,
+    centred,
+    moments,
     acc,
     alpha,
     direct,
@@ -159,6 +165,39 @@
         for m in range(8):
             window[2, k, 2, m : m + 1, :] = flags[4 * m + k : 4 * m + k + 1, :]
 
+    def place(row):
+        return EVERY.index(row)
+
+    def widen(row, col):
+        for c in range(2):
+            for k in range(6):
+                line = window[row, col, c, k : k + 1, :]
+                wide[row, col, c, k] = jnp.broadcast_to(line, (SUBS, LANES))
+
+    def widen_own(col, carry):
+        widen(2, col)
+        return carry
+
+    def widen_rest(index, carry):
+        row = index // 4
+        widen(row + row // 2, index % 4)
+        return carry
+
+    pl.semaphore_wait(barrier, len(partners))
+
+    def attr_copy(index, d):
+        return pltpu.make_async_remote_copy(
+            src_ref=window.at[2],
+            dst_ref=window.at[2 - d],
+            send_sem=send_sem.at[index],
+            recv_sem=recv_sem.at[index],
+            device_id=(at_space(d), pr),
+            device_id_type=MESH,
+        )
+
+    for index, d in enumerate(NEAR):
+        attr_copy(index, d).start()
+
     for a in range(2):
         for c in range(2):
             turned = window[2, a + 1, c].T
@@ -170,40 +209,29 @@
                 column[a, k, c * half : (c + 1) * half] = values.reshape(half, SUBS, LANES)
         alpha[a, 6:8, :] = jnp.zeros((2, LANES), jnp.float32)
 
-    def place(row):
-        if isinstance(row, int) and row == 2:
-            return 4
-        return row - row // 3 if isinstance(row, int) else row - lax.div(row, 3)
-
-    def widen(row, col):
-        for c in range(2):
-            for k in range(6):
-                line = window[row, col, c, k : k + 1, :]
-                wide[row, col, c, k] = jnp.broadcast_to(line, (SUBS, LANES))
-
-    def widen_own(col, carry):
-        widen(2, col)
-        return carry
-
-    def widen_rest(index, carry):
-        row = index // 4
-        widen(row + row // 2, index % 4)
-        return carry
-
-    pl.semaphore_wait(barrier, len(partners))
-
-    def attr_copy(index, d):
-        return pltpu.make_async_remote_copy(
-            src_ref=window.at[2],
-            dst_ref=window.at[2 - d],
-            send_sem=send_sem.at[index],
-            recv_sem=recv_sem.at[index],
-            device_id=(at_space(d), pr),
-            device_id_type=MESH,
+    sublane = lax.broadcasted_iota(jnp.int32, (SUBS, LANES), 0)
+    fourth = lax.rem(sublane, 4)
+
+    def choose(x, y, z, other):
+        return jnp.where(
+            fourth == 0, x, jnp.where(fourth == 1, y, jnp.where(fourth == 2, z, other))
         )
 
-    for index, d in enumerate(NEAR):
-        attr_copy(index, d).start()
+    def centre(a):
+        mean = jnp.sum(window[2, a + 1, 0] + window[2, a + 1, 1], axis=1, keepdims=True) / BLK
+        return [jnp.broadcast_to(mean[k : k + 1, :], (SUBS, LANES)) for k in range(3)]
+
+    def set_apart():
+        for a in range(2):
+            middle = centre(a)
+            for step in range(3):
+                for index, row in enumerate(DISTANT):
+                    for c in range(2):
+                        for k in range(3):
+                            apart[a, step, index, c, k] = wide[row, a + step, c, k] - middle[k]
+            for c in range(2):
+                own = [wide[2, a + 1, c, k] - middle[k] for k in range(3)]
+                centred[a, c] = choose(*own, -1.0)
 
     def weigh(a, row, step):
         slot = a * 15 + row * 3 + step
@@ -217,6 +245,7 @@
         line = window[min(row, 2), col, 2, entry : entry + 1, :]
         weight[slot, 0] = jnp.broadcast_to(line, (SUBS, LANES))
         weight[slot, 1] = jnp.broadcast_to(line * ROOT_THREE, (SUBS, LANES))
+        weight[slot, 2] = jnp.broadcast_to(line * 3.0, (SUBS, LANES))
 
     def build(a, part, row, step, c, totals, itself, masked):
         def far(line):
@@ -236,25 +265,33 @@
         fifth = (third + damping * decayed) * inverse
         tile = a * 15 + row * 3 + step
         three = (third * (inverse_sq * inverse)) * weight[tile, 0]
-        root = (fifth * lax.rsqrt(fifth)) * (inverse_sq * weight[tile, 1])
-        index = tile * 2 + c
-        coef[index, 0, part] = rx * root
-        coef[index, 1, part] = ry * root
-        coef[index, 2, part] = rz * root
+        rows = pl.ds(pl.multiple_of(part.start * SUBS, BUILD * SUBS), BUILD * SUBS)
+
+        def keep(matrices, value, lanes):
+            flat = value.reshape(BUILD * SUBS, LANES)
+            high = flat.astype(jnp.bfloat16)
+            low = (flat - high.astype(jnp.float32)).astype(jnp.bfloat16)
+            matrices[a, 2 * c, rows, lanes] = high
+            matrices[a, 2 * c + 1, rows, lanes] = low
+
+        if row in DISTANT:
+            five = (fifth * (inverse_sq * inverse_sq)) * weight[tile, 2]
+            lane = (step * 2 + DISTANT.index(row)) * LANES
+            keep(fives, five, slice(lane, lane + LANES))
+        else:
+            root = (fifth * lax.rsqrt(fifth)) * (inverse_sq * weight[tile, 1])
+            index = tile * 2 + c
+            coef[index, 0, part] = rx * root
+            coef[index, 1, part] = ry * root
+            coef[index, 2, part] = rz * root
         if itself:
             shape = (BUILD, SUBS, LANES)
             own = lax.broadcasted_iota(jnp.int32, shape, 0) * SUBS + part.start * SUBS
             own = own + lax.broadcasted_iota(jnp.int32, shape, 1)
             other = lax.broadcasted_iota(jnp.int32, shape, 2) + c * LANES
             three = jnp.where(own == other, 0.0, three)
-        flat = three.reshape(BUILD * SUBS, LANES)
-        high = flat.astype(jnp.bfloat16)
-        low = (flat - high.astype(jnp.float32)).astype(jnp.bfloat16)
-        first = pl.multiple_of(part.start * SUBS, BUILD * SUBS)
-        rows = pl.ds(first, BUILD * SUBS)
-        lanes = pl.ds(pl.multiple_of((step * 5 + place(row)) * LANES, LANES), LANES)
-        cubes[a, 2 * c, rows, lanes] = high
-        cubes[a, 2 * c + 1, rows, lanes] = low
+        lane = (step * 5 + place(row)) * LANES
+        keep(cubes, three, slice(lane, lane + LANES))
         charged = three * far(CHARGE)
         if masked:
             charged = jnp.where(column[a, GROUP, part] != far(GROUP), charged, 0.0)
@@ -284,6 +321,18 @@
             less = [
                 cubed[a, c, 0:8] + cubed[a, c, 8:16] + cubed[a, c, 16:24] for c in range(2)
             ]
+            expanded = []
+            for c in range(2):
+                lanes = slice(c * LANES, (c + 1) * LANES)
+                sums = []
+                for half in range(2):
+                    first = half * SUBS
+                    piece = [fived[a, first + 16 * m : first + 16 * m + 8, lanes] for m in range(3)]
+                    terms = (piece[0] + piece[1] + piece[2]) * centred[a, c]
+                    for quarter in range(2):
+                        rows = terms[4 * quarter : 4 * quarter + 4, :]
+                        sums.append(jnp.sum(rows, axis=0, keepdims=True))
+                expanded.append(sums)
         parts = []
         for k in range(3):
             for c in range(2):
@@ -295,6 +344,8 @@
                     part = part - (
                         less[0][2 * k : 2 * k + 1, lanes] + less[1][2 * k + 1 : 2 * k + 2, lanes]
                     )
+                    own = centred[a, c][k : k + 1, :]
+                    part = part + (own * expanded[c][0] - expanded[c][k + 1])
                 parts.append(part)
         parts.append(jnp.zeros((2, LANES), jnp.float32))
         return jnp.concatenate(parts, axis=0)
@@ -344,22 +395,18 @@
             for row in (0, 1):
                 weigh(a, row, step)
     lax.fori_loop(0, 16, widen_rest, 0)
+    set_apart()
 
     def build_rest(a, carry):
         def one_group(group, inner):
             part = pl.ds(group * BUILD, BUILD)
 
-            def one_row(row, totals, masked):
+            totals = load_acc(a, part)
+            for row in OTHERS:
                 for step in range(3):
                     for c in range(2):
-                        totals = build(
-                            a, part, row, step, c, totals, False, step == masked
-                        )
-                return totals
-
-            totals = load_acc(a, part)
-            totals = lax.fori_loop(0, 2, functools.partial(one_row, masked=0), totals)
-            totals = lax.fori_loop(3, 5, functools.partial(one_row, masked=2), totals)
+                        masked = (row, step) in ((1, 0), (3, 2))
+                        totals = build(a, part, row, step, c, totals, False, masked)
             store_acc(a, part, totals)
             return inner
 
@@ -377,17 +424,39 @@
 
     lax.fori_loop(0, 2, build_rest, 0)
 
+    def thirds(value):
+        high = value.astype(jnp.bfloat16).astype(jnp.float32)
+        rest = value - high
+        middle = rest.astype(jnp.bfloat16).astype(jnp.float32)
+        return [high, middle, rest - middle]
+
     def take(n, row, col):
         tile = vec[n, row, col]
-        for m in range(6):
-            spread[row, col, m] = jnp.broadcast_to(tile[m : m + 1, :], (SUBS, LANES))
-        high = tile.astype(jnp.bfloat16).astype(jnp.float32)
-        rest = tile - high
-        middle = rest.astype(jnp.bfloat16).astype(jnp.float32)
-        low = rest - middle
-        parts = jnp.concatenate([high, middle, low, jnp.zeros_like(low)], axis=0)
-        lanes = pl.ds((col * 5 + place(row)) * LANES, LANES)
-        pieces[:, lanes] = parts.astype(jnp.bfloat16)
+        lines = [jnp.broadcast_to(tile[m : m + 1, :], (SUBS, LANES)) for m in range(6)]
+        parts = jnp.concatenate(thirds(tile) + [jnp.zeros_like(tile)], axis=0)
+        lane = (col * 5 + place(row)) * LANES
+        pieces[:, lane : lane + LANES] = parts.astype(jnp.bfloat16)
+        if row not in DISTANT:
+            for m in range(6):
+                spread[row, col, m] = lines[m]
+            return
+        index = DISTANT.index(row)
+        for a in range(2):
+            step = col - a
+            if not 0 <= step < 3:
+                continue
+            for c in range(2):
+                x, y, z = (apart[a, step, index, c, k] for k in range(3))
+                vx, vy, vz = (lines[2 * k + c] for k in range(3))
+                four = choose(vx, vy, vz, x * vx + y * vy + z * vz)
+                upper = four * jnp.where(sublane < 4, 1.0, x)
+                lower = four * jnp.where(sublane < 4, y, z)
+                uppers, lowers = thirds(upper), thirds(lower)
+                parts = [value for pair in zip(uppers, lowers) for value in pair]
+                lane = (step * 2 + index) * LANES
+                moments[a, c, :, lane : lane + LANES] = jnp.concatenate(parts, axis=0).astype(
+                    jnp.bfloat16
+                )
 
     def ready(n, col):
         for index, (far, d) in enumerate(HALO):
@@ -395,33 +464,38 @@
                 halo_copy(n, index).wait()
                 take(n, 2 - d, col)
 
-    def strips(a, steps, rows, fresh):
-        first, last = (place(rows[0]), place(rows[-1]) + 1)
+    def strips(a, jobs, fresh):
         if fresh:
             cubed[a] = jnp.zeros((2, 4 * SUBS, BLK), jnp.float32)
+            fived[a] = jnp.zeros((6 * SUBS, BLK), jnp.float32)
+
+        def times(left, right):
+            return lax.dot_general(
+                left, right, (((1,), (1,)), ((), ())), preferred_element_type=jnp.float32
+            )
 
         def one_group(group, carry):
             part = pl.ds(group * APPLY, APPLY)
             c = group // 2
-            product = None
-            for step in steps:
+            for step, rows in jobs:
                 own = (a + step) * 5
-                term = lax.dot_general(
+                first, last = place(rows[0]), place(rows[-1]) + 1
+                cubed[a, c] = cubed[a, c] + times(
                     pieces[:, (own + first) * LANES : (own + last) * LANES],
-                    cubes[
-                        a, group, :, (step * 5 + first) * LANES : (step * 5 + last) * LANES
-                    ],
-                    (((1,), (1,)), ((), ())),
-                    preferred_element_type=jnp.float32,
+                    cubes[a, group, :, (step * 5 + first) * LANES : (step * 5 + last) * LANES],
                 )
-                product = term if product is None else product + term
+                if rows != (2,):
+                    lanes = slice(step * 2 * LANES, (step + 1) * 2 * LANES)
+                    fived[a] = fived[a] + times(
+                        moments[a, c, :, lanes], fives[a, group, :, lanes]
+                    )
             totals = zeros(APPLY) if fresh else load_acc(a, part)
-            for step in steps:
+            for step, rows in jobs:
                 for row in rows:
                     for k in range(2):
-                        totals = apply(a, part, row, step, k, totals)
+                        if row not in DISTANT:
+                            totals = apply(a, part, row, step, k, totals)
             store_acc(a, part, totals)
-            cubed[a, c] = cubed[a, c] + product
             return carry
 
         lax.fori_loop(0, TILES // APPLY, one_group, 0)
@@ -438,19 +512,18 @@
     def sweep(n, carry):
         take(n, 2, 1)
         take(n, 2, 2)
-        strips(0, (1, 2), (2,), True)
-        strips(1, (0, 1), (2,), True)
+        strips(0, [(1, (2,)), (2, (2,))], True)
+        strips(1, [(0, (2,)), (1, (2,))], True)
         ready(n, 1)
-        strips(0, (1,), OTHERS, False)
-        strips(1, (0,), OTHERS, False)
+        strips(0, [(1, OTHERS)], False)
+        strips(1, [(0, OTHERS)], False)
         ready(n, 2)
-        strips(1, (1,), OTHERS, False)
-        strips(0, (2,), OTHERS, False)
+        strips(1, [(1, OTHERS)], False)
         ready(n, 0)
-        strips(0, (0,), EVERY, False)
+        strips(0, [(2, OTHERS), (0, EVERY)], False)
         finish(n, 0)
         ready(n, 3)
-        strips(1, (2,), EVERY, False)
+        strips(1, [(2, EVERY)], False)
         finish(n, 1)
         return carry
 
@@ -560,10 +633,15 @@
             pltpu.VMEM((5, 4, 3, SUBS, LANES), jnp.float32),
             pltpu.VMEM((5, 4, 2, 6, SUBS, LANES), jnp.float32),
             pltpu.VMEM((2, 5, TILES, SUBS, LANES), jnp.float32),
-            pltpu.VMEM((30, 2, SUBS, LANES), jnp.float32),
+            pltpu.VMEM((30, 3, SUBS, LANES), jnp.float32),
             pltpu.VMEM((60, 3, TILES, SUBS, LANES), jnp.float32),
             pltpu.VMEM((2, 4, BLK, 15 * LANES), jnp.bfloat16),
             pltpu.VMEM((2, 2, 4 * SUBS, BLK), jnp.float32),
+            pltpu.VMEM((2, 4, BLK, 6 * LANES), jnp.bfloat16),
+            pltpu.VMEM((2, 6 * SUBS, BLK), jnp.float32),
+            pltpu.VMEM((2, 3, 2, 2, 3, SUBS, LANES), jnp.float32),
+            pltpu.VMEM((2, 2, SUBS, LANES), jnp.float32),
+            pltpu.VMEM((2, 2, 6 * SUBS, 6 * LANES), jnp.bfloat16),
             pltpu.VMEM((2, 3, TILES, SUBS, LANES), jnp.float32),
             pltpu.VMEM((2, 8, LANES), jnp.float32),
             pltpu.VMEM((2, 8, LANES), jnp.float32),

time: 82.1 us -> 82.4 us (level)
  no operation moved by 1% of the time
where the time goes in v5:
time: 82.4 us; the launch traced here: 81.6 us
  Pallas kernels  79.1 us (96%)
  between operations  1.29 us (2%)
  local copies, waits for them, and re-layouts  1.2 us (1%)
    pallas_call x1, Pallas kernels, on_device(): pl.pallas_call(functools.partial(kernel, spaces, pairs, span_y), out_shap...  79.1 us

profile of v5, /device:TPU:1, one launch (start us, length us, event | category | flops | bytes accessed | tf_op | source)
XLA Modules:
  0.0 81.6 jit_solution(3385644186941353563)
XLA Ops:
  1.3 79.1 %shard_map.77 = (f32[3,512]{1,0:T(4,128)S(1)}, f32[3,512]{1,0:T(4,128)S(1)}) custom-call(f32[3,2048]{1,0:T(4,128)} %positions_ref.1, f32[1,2048]{1,0:T(1,128)} %bitcast.6, f32[1,2048]{1,0:T(1,128)} %bitcast.7, s32[1,2048]{1,0:T(1,128)} %bitcast.8, s32[2,64]{1,0:T(2,128)} %bitcast.9, s32[1]{0:T(128)S(6)} %copy.10.count_ref), custom_call_target="tpu_custom_call" | custom-call | tf_op jit(solution)/shard_map/pallas_call | solution.py:621
  80.4 0.6 copy.11
  81.0 0.6 copy.12

commit v6 on v5

--- a/solution.py
+++ b/solution.py
@@ -22,9 +22,8 @@
 MESH = pl.DeviceIdType.MESH
 
 NEAR = [-2, -1, 1, 2]
-REACH = [-2, 2, -1, 1, 0]
-TARGETS = {1: (0, 0, NEAR), 3: (0, -1, REACH), 2: (1, 0, NEAR), 0: (1, 1, REACH)}
-HALO = [(column, d) for column in (1, 3, 2, 0) for d in TARGETS[column][2]]
+SEAT = {1: 0, 2: 1, 0: 2, 3: 3}
+COPIES = 2 + 2 * len(NEAR)
 X, Y, Z, GROUP, ROOT, CHARGE = range(6)
 OTHERS = (0, 1, 3, 4)
 EVERY = OTHERS + (2,)
@@ -121,7 +120,7 @@
     ]
 
     barrier = pltpu.get_barrier_semaphore()
-    partners = [(at_space(d), at_pair(e)) for d in REACH for e in (-1, 0, 1) if (d, e) != (0, 0)]
+    partners = [(at_space(d), pr) for d in NEAR]
     for members, _ in stages:
         partners = partners + members
     for partner in partners:
@@ -352,23 +351,38 @@
 
     base = len(NEAR)
 
-    def halo_copy(n, index):
-        col, d = HALO[index]
-        block, e, _ = TARGETS[col]
-        number = base + n * len(HALO) + index
+    def remote(source, target, number, device):
         return pltpu.make_async_remote_copy(
-            src_ref=vec.at[n, 2, block + 1],
-            dst_ref=vec.at[n, 2 - d, col],
+            src_ref=source,
+            dst_ref=target,
             send_sem=send_sem.at[number],
             recv_sem=recv_sem.at[number],
-            device_id=(at_space(d), at_pair(e)),
+            device_id=device,
             device_id_type=MESH,
         )
 
+    def beside(n, block):
+        target = vec.at[n, 2, SEAT[0 if block else 3]]
+        device = (sp, at_pair(1 if block else -1))
+        return remote(vec.at[n, 2, block], target, base + n * COPIES + block, device)
+
+    def across(n, half):
+        seats = pl.ds(2 * half, 2)
+        return [
+            remote(
+                vec.at[n, 2, seats],
+                vec.at[n, 2 - d, seats],
+                base + n * COPIES + 2 + half * len(NEAR) + index,
+                (at_space(d), pr),
+            )
+            for index, d in enumerate(NEAR)
+        ]
+
     def send(n, block):
-        for index, (col, _) in enumerate(HALO):
-            if TARGETS[col][0] == block:
-                halo_copy(n, index).start()
+        beside(n, block).start()
+        if block == 1:
+            for copy in across(n, 0):
+                copy.start()
 
     for a in range(2):
         for step in range(3):
@@ -413,7 +427,7 @@
         lax.fori_loop(0, TILES // BUILD, one_group, 0)
         value = summed(a, False)
         direct[a] = value
-        vec[0, 2, a + 1] = value * alpha[a]
+        vec[0, 2, a] = value * alpha[a]
         for block in range(2):
 
             @pl.when(a == block)
@@ -431,7 +445,7 @@
         return [high, middle, rest - middle]
 
     def take(n, row, col):
-        tile = vec[n, row, col]
+        tile = vec[n, row, SEAT[col]]
         lines = [jnp.broadcast_to(tile[m : m + 1, :], (SUBS, LANES)) for m in range(6)]
         parts = jnp.concatenate(thirds(tile) + [jnp.zeros_like(tile)], axis=0)
         lane = (col * 5 + place(row)) * LANES
@@ -458,12 +472,6 @@
                     jnp.bfloat16
                 )
 
-    def ready(n, col):
-        for index, (far, d) in enumerate(HALO):
-            if far == col:
-                halo_copy(n, index).wait()
-                take(n, 2 - d, col)
-
     def strips(a, jobs, fresh):
         if fresh:
             cubed[a] = jnp.zeros((2, 4 * SUBS, BLK), jnp.float32)
@@ -503,7 +511,7 @@
     def finish(n, a):
         value = summed(a, True)
         field[n, a] = value
-        vec[n + 1, 2, a + 1] = value * alpha[a]
+        vec[n + 1, 2, a] = value * alpha[a]
 
         @pl.when(n + 1 < SWEEPS)
         def _():
@@ -514,16 +522,25 @@
         take(n, 2, 2)
         strips(0, [(1, (2,)), (2, (2,))], True)
         strips(1, [(0, (2,)), (1, (2,))], True)
-        ready(n, 1)
-        strips(0, [(1, OTHERS)], False)
-        strips(1, [(0, OTHERS)], False)
-        ready(n, 2)
-        strips(1, [(1, OTHERS)], False)
-        ready(n, 0)
-        strips(0, [(2, OTHERS), (0, EVERY)], False)
+        for block in range(2):
+            beside(n, block).wait_recv()
+        for copy in across(n, 1):
+            copy.start()
+        take(n, 2, 0)
+        take(n, 2, 3)
+        for index, copy in enumerate(across(n, 0)):
+            copy.wait_recv()
+            for col in (1, 2):
+                take(n, 2 - NEAR[index], col)
+        strips(0, [(1, OTHERS), (2, OTHERS), (0, (2,))], False)
+        strips(1, [(0, OTHERS), (1, OTHERS), (2, (2,))], False)
+        for index, copy in enumerate(across(n, 1)):
+            copy.wait_recv()
+            for col in (0, 3):
+                take(n, 2 - NEAR[index], col)
+        strips(0, [(0, OTHERS)], False)
         finish(n, 0)
-        ready(n, 3)
-        strips(1, [(2, EVERY)], False)
+        strips(1, [(2, OTHERS)], False)
         finish(n, 1)
         return carry
 
@@ -535,24 +552,29 @@
         lines.append(jnp.sum(product, axis=0, keepdims=True))
     lines.append(jnp.zeros((16 - len(GRAM), LANES), jnp.float32))
     total = jnp.concatenate(lines, axis=0)
-    first = base + SWEEPS * len(HALO)
+    first = base + SWEEPS * COPIES
+    pending = []
     for stage, (members, mine) in enumerate(stages):
         gram[stage, mine] = total
-        copies = []
-        for index, member in enumerate(members):
-            copies.append(
-                pltpu.make_async_remote_copy(
-                    src_ref=gram.at[stage, mine],
-                    dst_ref=gram.at[stage, mine],
-                    send_sem=send_sem.at[first + index],
-                    recv_sem=recv_sem.at[first + index],
-                    device_id=member,
-                    device_id_type=MESH,
-                )
-            )
-            copies[-1].start()
+        copies = [
+            remote(gram.at[stage, mine], gram.at[stage, mine], first + index, member)
+            for index, member in enumerate(members)
+        ]
         for copy in copies:
-            copy.wait()
+            copy.start()
+        if stage == 0:
+
+            def sent(n, carry):
+                for copy in [beside(n, 0), beside(n, 1)] + across(n, 0) + across(n, 1):
+                    copy.wait_send()
+                return carry
+
+            lax.fori_loop(0, SWEEPS, sent, 0)
+        for copy in pending:
+            copy.wait_send()
+        pending = copies
+        for copy in copies:
+            copy.wait_recv()
         first += len(members)
         total = gram[stage, 0]
         for index in range(1, len(members) + 1):
@@ -609,12 +631,14 @@
                 lanes = slice(a * BLK + c * LANES, a * BLK + (c + 1) * LANES)
                 dip_ref[k : k + 1, lanes] = moved[2 * k + c : 2 * k + c + 1, :]
                 res_ref[k : k + 1, lanes] = left[2 * k + c : 2 * k + c + 1, :]
+    for copy in pending:
+        copy.wait_send()
 
 
 def on_device(spaces, pairs, span_y, positions, polarizability, charges, groups, pair_list, tile_count):
     atoms = positions.shape[1]
     listed = pair_list.shape[1]
-    copies = len(NEAR) + SWEEPS * len(HALO) + 2 * pairs + span_y + spaces // (2 * span_y) - 3
+    copies = len(NEAR) + SWEEPS * COPIES + 2 * pairs + span_y + spaces // (2 * span_y) - 3
     share = jax.ShapeDtypeStruct((3, 2 * BLK), jnp.float32)
     vmem = pl.BlockSpec(memory_space=pltpu.VMEM)
     hbm = pl.BlockSpec(memory_space=pltpu.HBM)

time: 82.4 us -> 85.5 us (1.038)
  Pallas kernels: 79.1 us -> 82 us
    pallas_call x1, Pallas kernels: 79.1 us -> 82 us  [on_device(): pl.pallas_call(functools.partial(kernel, spaces, pairs, span_y), out_shap...]
where the time goes in v6:
time: 85.5 us; the launch traced here: 84.5 us
  Pallas kernels  82 us (96%)
  between operations  1.29 us (2%)
  local copies, waits for them, and re-layouts  1.2 us (1%)
    pallas_call x1, Pallas kernels, on_device(): pl.pallas_call(functools.partial(kernel, spaces, pairs, span_y), out_shap...  82 us

profile of v6, /device:TPU:1, one launch (start us, length us, event | category | flops | bytes accessed | tf_op | source)
XLA Modules:
  0.0 84.5 jit_solution(4994069608748806744)
XLA Ops:
  1.3 82.0 %shard_map.77 = (f32[3,512]{1,0:T(4,128)S(1)}, f32[3,512]{1,0:T(4,128)S(1)}) custom-call(f32[3,2048]{1,0:T(4,128)} %positions_ref.1, f32[1,2048]{1,0:T(1,128)} %bitcast.6, f32[1,2048]{1,0:T(1,128)} %bitcast.7, s32[1,2048]{1,0:T(1,128)} %bitcast.8, s32[2,64]{1,0:T(2,128)} %bitcast.9, s32[1]{0:T(128)S(6)} %copy.10.count_ref), custom_call_target="tpu_custom_call" | custom-call | tf_op jit(solution)/shard_map/pallas_call | solution.py:645
  83.3 0.6 copy.11
  83.9 0.6 copy.12

commit v7 on v4

--- a/solution.py
+++ b/solution.py
@@ -159,6 +159,39 @@
         for m in range(8):
             window[2, k, 2, m : m + 1, :] = flags[4 * m + k : 4 * m + k + 1, :]
 
+    def place(row):
+        return EVERY.index(row)
+
+    def widen(row, col):
+        for c in range(2):
+            for k in range(6):
+                line = window[row, col, c, k : k + 1, :]
+                wide[row, col, c, k] = jnp.broadcast_to(line, (SUBS, LANES))
+
+    def widen_own(col, carry):
+        widen(2, col)
+        return carry
+
+    def widen_rest(index, carry):
+        row = index // 4
+        widen(row + row // 2, index % 4)
+        return carry
+
+    pl.semaphore_wait(barrier, len(partners))
+
+    def attr_copy(index, d):
+        return pltpu.make_async_remote_copy(
+            src_ref=window.at[2],
+            dst_ref=window.at[2 - d],
+            send_sem=send_sem.at[index],
+            recv_sem=recv_sem.at[index],
+            device_id=(at_space(d), pr),
+            device_id_type=MESH,
+        )
+
+    for index, d in enumerate(NEAR):
+        attr_copy(index, d).start()
+
     for a in range(2):
         for c in range(2):
             turned = window[2, a + 1, c].T
@@ -169,41 +202,6 @@
                 half = LANES // SUBS
                 column[a, k, c * half : (c + 1) * half] = values.reshape(half, SUBS, LANES)
         alpha[a, 6:8, :] = jnp.zeros((2, LANES), jnp.float32)
-
-    def place(row):
-        if isinstance(row, int) and row == 2:
-            return 4
-        return row - row // 3 if isinstance(row, int) else row - lax.div(row, 3)
-
-    def widen(row, col):
-        for c in range(2):
-            for k in range(6):
-                line = window[row, col, c, k : k + 1, :]
-                wide[row, col, c, k] = jnp.broadcast_to(line, (SUBS, LANES))
-
-    def widen_own(col, carry):
-        widen(2, col)
-        return carry
-
-    def widen_rest(index, carry):
-        row = index // 4
-        widen(row + row // 2, index % 4)
-        return carry
-
-    pl.semaphore_wait(barrier, len(partners))
-
-    def attr_copy(index, d):
-        return pltpu.make_async_remote_copy(
-            src_ref=window.at[2],
-            dst_ref=window.at[2 - d],
-            send_sem=send_sem.at[index],
-            recv_sem=recv_sem.at[index],
-            device_id=(at_space(d), pr),
-            device_id_type=MESH,
-        )
-
-    for index, d in enumerate(NEAR):
-        attr_copy(index, d).start()
 
     def weigh(a, row, step):
         slot = a * 15 + row * 3 + step
@@ -338,7 +336,7 @@
 
     lax.fori_loop(0, 2 * (TILES // BUILD), build_own, 0)
     for index, d in enumerate(NEAR):
-        attr_copy(index, d).wait()
+        attr_copy(index, d).wait_recv()
     for a in range(2):
         for step in range(3):
             for row in (0, 1):
@@ -349,17 +347,12 @@
         def one_group(group, inner):
             part = pl.ds(group * BUILD, BUILD)
 
-            def one_row(row, totals, masked):
+            totals = load_acc(a, part)
+            for row in OTHERS:
                 for step in range(3):
                     for c in range(2):
-                        totals = build(
-                            a, part, row, step, c, totals, False, step == masked
-                        )
-                return totals
-
-            totals = load_acc(a, part)
-            totals = lax.fori_loop(0, 2, functools.partial(one_row, masked=0), totals)
-            totals = lax.fori_loop(3, 5, functools.partial(one_row, masked=2), totals)
+                        masked = (row, step) in ((1, 0), (3, 2))
+                        totals = build(a, part, row, step, c, totals, False, masked)
             store_acc(a, part, totals)
             return inner
 
@@ -392,7 +385,7 @@
     def ready(n, col):
         for index, (far, d) in enumerate(HALO):
             if far == col:
-                halo_copy(n, index).wait()
+                halo_copy(n, index).wait_recv()
                 take(n, 2 - d, col)
 
     def strips(a, steps, rows, fresh):
@@ -463,6 +456,7 @@
     lines.append(jnp.zeros((16 - len(GRAM), LANES), jnp.float32))
     total = jnp.concatenate(lines, axis=0)
     first = base + SWEEPS * len(HALO)
+    pending = [attr_copy(index, d) for index, d in enumerate(NEAR)]
     for stage, (members, mine) in enumerate(stages):
         gram[stage, mine] = total
         copies = []
@@ -478,8 +472,19 @@
                 )
             )
             copies[-1].start()
+        if stage == 0:
+
+            def sent(n, carry):
+                for index in range(len(HALO)):
+                    halo_copy(n, index).wait_send()
+                return carry
+
+            lax.fori_loop(0, SWEEPS, sent, 0)
+        for copy in pending:
+            copy.wait_send()
+        pending = copies
         for copy in copies:
-            copy.wait()
+            copy.wait_recv()
         first += len(members)
         total = gram[stage, 0]
         for index in range(1, len(members) + 1):
@@ -536,6 +541,8 @@
                 lanes = slice(a * BLK + c * LANES, a * BLK + (c + 1) * LANES)
                 dip_ref[k : k + 1, lanes] = moved[2 * k + c : 2 * k + c + 1, :]
                 res_ref[k : k + 1, lanes] = left[2 * k + c : 2 * k + c + 1, :]
+    for copy in pending:
+        copy.wait_send()
 
 
 def on_device(spaces, pairs, span_y, positions, polarizability, charges, groups, pair_list, tile_count):

time: 82.1 us -> 80.8 us (0.984)
  Pallas kernels: 78.9 us -> 77.5 us
    pallas_call x1, Pallas kernels: 78.9 us -> 77.5 us  [on_device(): pl.pallas_call(functools.partial(kernel, spaces, pairs, span_y), out_shap...]
where the time goes in v7:
time: 80.8 us; the launch traced here: 80 us
  Pallas kernels  77.5 us (96%)
  between operations  1.29 us (2%)
  local copies, waits for them, and re-layouts  1.2 us (1%)
    pallas_call x1, Pallas kernels, on_device(): pl.pallas_call(functools.partial(kernel, spaces, pairs, span_y), out_shap...  77.5 us

profile of v7, /device:TPU:1, one launch (start us, length us, event | category | flops | bytes accessed | tf_op | source)
XLA Modules:
  0.0 80.0 jit_solution(13527992979874537936)
XLA Ops:
  1.3 77.5 %shard_map.77 = (f32[3,512]{1,0:T(4,128)S(1)}, f32[3,512]{1,0:T(4,128)S(1)}) custom-call(f32[3,2048]{1,0:T(4,128)} %positions_ref.1, f32[1,2048]{1,0:T(1,128)} %bitcast.6, f32[1,2048]{1,0:T(1,128)} %bitcast.7, s32[1,2048]{1,0:T(1,128)} %bitcast.8, s32[2,64]{1,0:T(2,128)} %bitcast.9, s32[1]{0:T(128)S(6)} %copy.10.count_ref), custom_call_target="tpu_custom_call" | custom-call | tf_op jit(solution)/shard_map/pallas_call | solution.py:555
  78.8 0.6 copy.11
  79.4 0.6 copy.12

commit v8 on v7

--- a/solution.py
+++ b/solution.py
@@ -125,13 +125,13 @@
         load.wait()
 
     slot, partner = listing[0:1, :], listing[1:2, :]
-    row_step = partner // BPD - sp
-    col_step = (partner % BPD - slot + (BPD + 1)) % BPD - 1
+    row_step = (partner >> 3) - sp
+    col_step = (((partner & 7) - slot + (BPD + 1)) & 7) - 1
     kind = jnp.where(row_step == 0, col_step, row_step * 3 + col_step)
     entry = lax.broadcasted_iota(jnp.int32, slot.shape, 1)
     key = jnp.where(entry < count_ref[0], kind * BPD + slot, -1)
     wanted = lax.broadcasted_iota(jnp.int32, (32, slot.shape[1]), 0)
-    wanted = (wanted // 4) * BPD + (2 * pr + (BPD - 1) + wanted % 4) % BPD
+    wanted = (wanted >> 2) * BPD + ((2 * pr + (BPD - 1) + (wanted & 3)) & 7)
     found = jnp.max((key == wanted).astype(jnp.float32), axis=1, keepdims=True)
     flags[...] = jnp.broadcast_to(found, (32, LANES))
 
@@ -172,11 +172,6 @@
         widen(2, col)
         return carry
 
-    def widen_rest(index, carry):
-        row = index // 4
-        widen(row + row // 2, index % 4)
-        return carry
-
     pl.semaphore_wait(barrier, len(partners))
 
     def attr_copy(index, d):
@@ -189,8 +184,8 @@
             device_id_type=MESH,
         )
 
-    for index, d in enumerate(NEAR):
-        attr_copy(index, d).start()
+    for index in (1, 2, 0, 3):
+        attr_copy(index, NEAR[index]).start()
 
     for a in range(2):
         for c in range(2):
@@ -335,28 +330,41 @@
         return carry
 
     lax.fori_loop(0, 2 * (TILES // BUILD), build_own, 0)
-    for index, d in enumerate(NEAR):
-        attr_copy(index, d).wait_recv()
-    for a in range(2):
-        for step in range(3):
-            for row in (0, 1):
-                weigh(a, row, step)
-    lax.fori_loop(0, 16, widen_rest, 0)
-
-    def build_rest(a, carry):
-        def one_group(group, inner):
+
+    def build_rows(a, rows):
+        def one_group(group, carry):
             part = pl.ds(group * BUILD, BUILD)
-
             totals = load_acc(a, part)
-            for row in OTHERS:
+            for row in rows:
                 for step in range(3):
                     for c in range(2):
                         masked = (row, step) in ((1, 0), (3, 2))
                         totals = build(a, part, row, step, c, totals, False, masked)
             store_acc(a, part, totals)
-            return inner
+            return carry
 
         lax.fori_loop(0, TILES // BUILD, one_group, 0)
+
+    def arrived(rows):
+        for row in rows:
+            attr_copy(NEAR.index(2 - row), 2 - row).wait_recv()
+        for a in range(2):
+            for step in range(3):
+                weigh(a, min(rows), step)
+
+        def widen_rows(col, carry):
+            for row in rows:
+                widen(row, col)
+            return carry
+
+        lax.fori_loop(0, 4, widen_rows, 0)
+
+    def build_next(a, carry):
+        build_rows(a, (1, 3))
+        return carry
+
+    def build_last(a, carry):
+        build_rows(a, (0, 4))
         value = summed(a, False)
         direct[a] = value
         vec[0, 2, a + 1] = value * alpha[a]
@@ -368,7 +376,10 @@
 
         return carry
 
-    lax.fori_loop(0, 2, build_rest, 0)
+    arrived((1, 3))
+    lax.fori_loop(0, 2, build_next, 0)
+    arrived((0, 4))
+    lax.fori_loop(0, 2, build_last, 0)
 
     def take(n, row, col):
         tile = vec[n, row, col]

time: 80.8 us -> 79.5 us (0.984)
  Pallas kernels: 77.5 us -> 76.5 us
    pallas_call x1, Pallas kernels: 77.5 us -> 76.5 us  [on_device(): pl.pallas_call(functools.partial(kernel, spaces, pairs, span_y), out_shap...]
where the time goes in v8:
time: 79.5 us; the launch traced here: 79 us
  Pallas kernels  76.5 us (96%)
  between operations  1.29 us (2%)
  local copies, waits for them, and re-layouts  1.2 us (2%)
    pallas_call x1, Pallas kernels, on_device(): pl.pallas_call(functools.partial(kernel, spaces, pairs, span_y), out_shap...  76.5 us

profile of v8, /device:TPU:1, one launch (start us, length us, event | category | flops | bytes accessed | tf_op | source)
XLA Modules:
  0.0 79.0 jit_solution(1351019543807741392)
XLA Ops:
  1.3 76.5 %shard_map.77 = (f32[3,512]{1,0:T(4,128)S(1)}, f32[3,512]{1,0:T(4,128)S(1)}) custom-call(f32[3,2048]{1,0:T(4,128)} %positions_ref.1, f32[1,2048]{1,0:T(1,128)} %bitcast.6, f32[1,2048]{1,0:T(1,128)} %bitcast.7, s32[1,2048]{1,0:T(1,128)} %bitcast.8, s32[2,64]{1,0:T(2,128)} %bitcast.9, s32[1]{0:T(128)S(6)} %copy.10.count_ref), custom_call_target="tpu_custom_call" | custom-call | tf_op jit(solution)/shard_map/pallas_call | solution.py:566
  77.8 0.6 copy.11
  78.4 0.6 copy.12
